TPU v7x, 256 devices: a whole 4x4x8 slice. The times are simulated.
256 devices in a mesh: section: 2 (over core), tensor: 16 (over y, x), dp: 8 (over z).
Axes of the slice: x: 4, y: 4, z: 8, core: 2. Of those that a mesh axis runs over, the one named last changes fastest.
Arguments:
- hidden_in: bfloat16 [8, 256, 6144], P('dp', None, 'tensor'), may hold values from -45 to 45
- doc_lengths: int32 [8, 4], P('dp'), may hold values from 1 to 128, 256 in all within a row
- w_qkv: bfloat16 [2, 6144, 18432], P('section', 'dp', 'tensor'), may hold values from -4 to 4
- w_out: bfloat16 [2, 6144, 6144], P('section', 'dp', 'tensor'), may hold values from -0.078125 to 0.078125
Outputs:
- layer_states: bfloat16 [2, 8, 256, 6144], P('section', 'dp', None, 'tensor')
Inputs may be any that keep to these rules, and one draw needn't show every extreme that they name: `doc_lengths`: each row gives the lengths of 4 packed documents in order, summing to 256.
All inputs are finite; a program needn't handle non-finite values.
Results may differ from a plain program's by a relative error of at most 0.0041.
Values may be sent and summed in bfloat16 or wider, within the bound.
A program may use at most 64 MiB of HBM per device.

v0:
```python
import math

import jax
import jax.numpy as jnp
from jax import lax
from jax.sharding import PartitionSpec as P

HD = 128


def shifted(array, axis, by):
    peers = lax.axis_size(axis)
    pairs = [(i, i + by) for i in range(peers) if 0 <= i + by < peers]
    return lax.ppermute(array, axis, pairs)


def normalize(values_rows):
    average = jnp.mean(values_rows, axis=-1, keepdims=True)
    centred = values_rows - average
    spread = jnp.mean(centred * centred, axis=-1, keepdims=True)
    return centred * lax.rsqrt(spread + 1e-05)


def local(hidden_in, doc_lengths, w_qkv, w_out):
    sections = lax.axis_size("section")
    my_section = lax.axis_index("section")
    seq_len = hidden_in.shape[1]
    feat_cols = hidden_in.shape[2]
    pieces = 4
    block = seq_len // pieces
    qkv_full, out_full = (
        lax.all_gather(w_qkv[0], "dp", axis=0, tiled=True),
        lax.all_gather(w_out[0], "dp", axis=0, tiled=True),
    )
    head_cols = qkv_full.shape[1] // 3
    heads_here = head_cols // HD
    score_scale = 1.0 / math.sqrt(HD)
    positions = jnp.arange(seq_len, dtype=jnp.int32)
    doc_ends = jnp.cumsum(doc_lengths[0])
    doc_of = jnp.sum((positions[:, None] >= doc_ends[None, :]).astype(jnp.int32), axis=1)
    own_rows = hidden_in[0]
    incoming = jnp.zeros((block, feat_cols), jnp.bfloat16)
    key_cache = jnp.zeros((seq_len, head_cols), jnp.bfloat16)
    value_cache = jnp.zeros((seq_len, head_cols), jnp.bfloat16)
    saved = jnp.zeros((seq_len, feat_cols), jnp.bfloat16)

    def attention(operands):
        whole, key_cache, value_cache, slot = operands
        normed = normalize(whole.astype(jnp.float32)).astype(jnp.bfloat16)
        projected = jnp.dot(normed, qkv_full, preferred_element_type=jnp.float32).astype(
            jnp.bfloat16
        )
        projected = projected.reshape(block, heads_here, 3, HD)
        query = projected[:, :, 0]
        fresh_keys = projected[:, :, 1].reshape(block, head_cols)
        fresh_values = projected[:, :, 2].reshape(block, head_cols)
        start = slot * block
        key_cache = lax.dynamic_update_slice_in_dim(key_cache, fresh_keys, start, 0)
        value_cache = lax.dynamic_update_slice_in_dim(value_cache, fresh_values, start, 0)
        query_pos = start + jnp.arange(block, dtype=jnp.int32)
        query_doc = lax.dynamic_slice_in_dim(doc_of, start, block, 0)
        allowed = (positions[None, :] <= query_pos[:, None]) & (
            doc_of[None, :] == query_doc[:, None]
        )
        keys_heads = key_cache.reshape(seq_len, heads_here, HD)
        values_heads = value_cache.reshape(seq_len, heads_here, HD)
        scores = (
            jnp.einsum("qhd,khd->hqk", query, keys_heads, preferred_element_type=jnp.float32)
            * score_scale
        )
        scores = jnp.where(allowed[None], scores, -1e30)
        row_max = jnp.max(scores, axis=-1, keepdims=True)
        weights_exp = jnp.exp(scores - row_max)
        softmax_out = (weights_exp / jnp.sum(weights_exp, axis=-1, keepdims=True)).astype(
            jnp.bfloat16
        )
        attended = jnp.einsum(
            "hqk,khd->qhd", softmax_out, values_heads, preferred_element_type=jnp.float32
        )
        return (attended.astype(jnp.bfloat16).reshape(block, head_cols), key_cache, value_cache)

    def resting(operands):
        whole, key_cache, value_cache, slot = operands
        return (jnp.zeros((block, head_cols), jnp.bfloat16), key_cache, value_cache)

    def project_out(operands):
        current, all_heads = operands
        update = jnp.dot(all_heads, out_full, preferred_element_type=jnp.float32)
        return (current.astype(jnp.float32) + update).astype(jnp.bfloat16)

    def pass_through(operands):
        current, all_heads = operands
        return current

    def advance(moment, carry):
        incoming, key_cache, value_cache, saved = carry
        index = moment - my_section
        active = (index >= 0) & (index < pieces)
        slot = jnp.clip(index, 0, pieces - 1)
        first_slot = jnp.clip(moment, 0, pieces - 1)
        fresh = lax.dynamic_slice_in_dim(own_rows, first_slot * block, block, 0)
        current = jnp.where(my_section == 0, fresh, incoming)
        whole = lax.all_gather(current, "tensor", axis=1, tiled=True)
        head_out, key_cache, value_cache = lax.cond(
            active, attention, resting, (whole, key_cache, value_cache, slot)
        )
        all_heads = lax.all_gather(head_out, "tensor", axis=1, tiled=True)
        result = lax.cond(active, project_out, pass_through, (current, all_heads))
        written = lax.dynamic_update_slice_in_dim(saved, result, slot * block, 0)
        saved = jnp.where(active, written, saved)
        incoming = shifted(result, "section", 1)
        return (incoming, key_cache, value_cache, saved)

    final_carry = lax.fori_loop(
        0, pieces + sections - 1, advance, (incoming, key_cache, value_cache, saved)
    )
    return final_carry[3][None, None]


def solution(mesh):
    return jax.shard_map(
        local,
        mesh=mesh,
        in_specs=(
            P("dp", None, "tensor"),
            P("dp", None),
            P("section", "dp", "tensor"),
            P("section", "dp", "tensor"),
        ),
        out_specs=P("section", "dp", None, "tensor"),
        check_vma=False,
    )
```

profile of v0, /device:TPU:1, one launch (start us, length us, event | category | flops | bytes accessed | tf_op | source)
XLA Modules:
  0.0 542.4 jit_solution(9494415282145935623)
XLA Ops:
  6.5 0.7 all-gather.7.cloned.1.call-update
  8.3 64.4 %all-gather.7.cloned.1.call-done = bf16[1,6144,384]{2,1,0:T(8,128)(2,1)} async-done(((bf16[1,768,384]{2,1,0:T(8,128)(2,1)}), bf16[1,6144,384]{2,1,0:T(8,128)(2,1)}) %all-gather.7.cloned.1.call-update) | async-done | bytes 4718608 | tf_op jit(solution)/shard_map/all_gather | solution.py:33
  72.7 148.6 %all-gather.5.cloned.1.call-done = bf16[1,6144,1152]{2,1,0:T(8,128)(2,1)} async-done(((bf16[1,768,1152]{2,1,0:T(8,128)(2,1)}), bf16[1,6144,1152]{2,1,0:T(8,128)(2,1)}) %all-gather.5.cloned.1.call-update) | async-done | bytes 14155792 | tf_op jit(solution)/shard_map/all_gather | solution.py:32
  221.4 313.5 %while.21 = (s32[]{:T(128)}, bf16[64,384]{1,0:T(8,128)(2,1)S(1)}, bf16[256,384]{0,1:T(8,128)(2,1)S(1)}, bf16[256,384]{0,1:T(8,128)(2,1)S(1)}, bf16[256,384]{1,0:...) while((s32[]{:T(128)}, bf16[64,384]{1,0:T(8,128)(2,1)S(1)}, ...), condition=%wide.region_11.12_spmd.clone, body=%wide.region_2.11_spmd.clone.sunk | while | flops 1237672704 | bytes 26632760 | solution.py:114
  221.4 0.8 dynamic-slice_select_fusion.2
  222.3 20.0 %all_gather.28 = bf16[64,6144]{1,0:T(8,128)(2,1)S(1)} all-gather(bf16[64,384]{1,0:T(8,128)(2,1)S(1)} %dynamic-slice_select_fusion.2), channel_id=1, replica_groups=mesh['section'=2,'tensor'=16,'dp'=8] {'tensor'}, dimensions={1}, use_global_device_ids=true | all-gather | bytes 835584 | tf_op jit(solution)/shard_map/while/body/eval_jaxpr/all_gather | solution.py:103
  242.3 18.4 %all_gather.29 = bf16[64,6144]{1,0:T(8,128)(2,1)S(1)} all-gather(bf16[64,384]{1,0:T(8,128)(2,1)S(1)} %get-tuple-element.437), channel_id=1, replica_groups=mesh['section'=2,'tensor'=16,'dp'=8] {'tensor'}, dimensions={1}, use_global_device_ids=true | all-gather | bytes 835584 | tf_op jit(solution)/shard_map/while/body/eval_jaxpr/all_gather | solution.py:107
  260.7 1.3 collective-permute-start
  262.0 25.4 %collective-permute-done = bf16[64,384]{1,0:T(8,128)(2,1)S(1)} collective-permute-done((bf16[64,384]{1,0:T(8,128)(2,1)S(1)}, bf16[64,384]{1,0:T(8,128)(2,1)S(1)}, u32[]{:S(2)}, u32[]{:S(2)}) %collective-permute-start) | collective-permute-done | bytes 49184 | tf_op jit(solution)/shard_map/while/body/eval_jaxpr/ppermute | solution.py:14
  287.4 0.8 dynamic-slice_select_fusion.2
  288.3 17.6 %all_gather.28 = bf16[64,6144]{1,0:T(8,128)(2,1)S(1)} all-gather(bf16[64,384]{1,0:T(8,128)(2,1)S(1)} %dynamic-slice_select_fusion.2), channel_id=1, replica_groups=mesh['section'=2,'tensor'=16,'dp'=8] {'tensor'}, dimensions={1}, use_global_device_ids=true | all-gather | bytes 835584 | tf_op jit(solution)/shard_map/while/body/eval_jaxpr/all_gather | solution.py:103
  305.9 10.6 %conditional.6 = (bf16[64,384]{1,0:T(8,128)(2,1)S(1)}, bf16[256,384]{0,1:T(8,128)(2,1)S(1)}, bf16[256,384]{0,1:T(8,128)(2,1)S(1)}) conditional(s32[]{:T(128)} %convert_element_type.61, (bf16[256,384]{0,1:T(8,128)(2,1)S(1)}, bf16[256,384]{0,1:T(8,128)(2,1)S(1)}) %tuple.64, (bf16[64,6144]{1,0:T(8,128)(2,1)S(1)}, bf16[6144,1152]{1,0:T(8,128)(2,1)}, ...), branch_computations={%region_3.3_spmd, %region_4.8_spmd} | conditional | flops 935560000 | bytes 18865236 | solution.py:104
  306.5 7.6 %convolution_convert_fusion = bf16[64,1152]{1,0:T(8,128)(2,1)S(1)} fusion(bf16[6144,1152]{1,0:T(8,128)(2,1)} %get-tuple-element.267, bf16[64,6144]{1,0:T(8,128)(2,1)S(1)} %get-tuple-element.266, f32[64]{0:T(128)S(1)} %add_rsqrt_fusion, f32[64]{0:T(128)S(1)} %broadcast_multiply_fusion), kind=kOutput, calls=%fused_computation.2 | convolution fusion | flops 907616256 | bytes 15090176 | tf_op jit(solution)/shard_map/while/body/eval_jaxpr/cond/branch_1_fun/dot_general | solution.py:50
  316.5 19.1 %all_gather.29 = bf16[64,6144]{1,0:T(8,128)(2,1)S(1)} all-gather(bf16[64,384]{1,0:T(8,128)(2,1)S(1)} %get-tuple-element.437), channel_id=1, replica_groups=mesh['section'=2,'tensor'=16,'dp'=8] {'tensor'}, dimensions={1}, use_global_device_ids=true | all-gather | bytes 835584 | tf_op jit(solution)/shard_map/while/body/eval_jaxpr/all_gather | solution.py:107
  335.7 3.2 conditional.7
  335.7 3.2 fusion.16
  338.8 1.3 collective-permute-start
  340.2 11.4 %collective-permute-done = bf16[64,384]{1,0:T(8,128)(2,1)S(1)} collective-permute-done((bf16[64,384]{1,0:T(8,128)(2,1)S(1)}, bf16[64,384]{1,0:T(8,128)(2,1)S(1)}, u32[]{:S(2)}, u32[]{:S(2)}) %collective-permute-start) | collective-permute-done | bytes 49184 | tf_op jit(solution)/shard_map/while/body/eval_jaxpr/ppermute | solution.py:14
  351.6 0.8 dynamic-slice_select_fusion.2
  352.4 18.1 %all_gather.28 = bf16[64,6144]{1,0:T(8,128)(2,1)S(1)} all-gather(bf16[64,384]{1,0:T(8,128)(2,1)S(1)} %dynamic-slice_select_fusion.2), channel_id=1, replica_groups=mesh['section'=2,'tensor'=16,'dp'=8] {'tensor'}, dimensions={1}, use_global_device_ids=true | all-gather | bytes 835584 | tf_op jit(solution)/shard_map/while/body/eval_jaxpr/all_gather | solution.py:103
  370.5 11.3 %conditional.6 = (bf16[64,384]{1,0:T(8,128)(2,1)S(1)}, bf16[256,384]{0,1:T(8,128)(2,1)S(1)}, bf16[256,384]{0,1:T(8,128)(2,1)S(1)}) conditional(s32[]{:T(128)} %convert_element_type.61, (bf16[256,384]{0,1:T(8,128)(2,1)S(1)}, bf16[256,384]{0,1:T(8,128)(2,1)S(1)}) %tuple.64, (bf16[64,6144]{1,0:T(8,128)(2,1)S(1)}, bf16[6144,1152]{1,0:T(8,128)(2,1)}, ...), branch_computations={%region_3.3_spmd, %region_4.8_spmd} | conditional | flops 935560000 | bytes 18865236 | solution.py:104
  371.1 7.6 %convolution_convert_fusion = bf16[64,1152]{1,0:T(8,128)(2,1)S(1)} fusion(bf16[6144,1152]{1,0:T(8,128)(2,1)} %get-tuple-element.267, bf16[64,6144]{1,0:T(8,128)(2,1)S(1)} %get-tuple-element.266, f32[64]{0:T(128)S(1)} %add_rsqrt_fusion, f32[64]{0:T(128)S(1)} %broadcast_multiply_fusion), kind=kOutput, calls=%fused_computation.2 | convolution fusion | flops 907616256 | bytes 15090176 | tf_op jit(solution)/shard_map/while/body/eval_jaxpr/cond/branch_1_fun/dot_general | solution.py:50
  379.2 0.8 dynamic_update_slice.7
  380.1 0.8 dynamic_update_slice.8
  381.8 18.0 %all_gather.29 = bf16[64,6144]{1,0:T(8,128)(2,1)S(1)} all-gather(bf16[64,384]{1,0:T(8,128)(2,1)S(1)} %get-tuple-element.437), channel_id=1, replica_groups=mesh['section'=2,'tensor'=16,'dp'=8] {'tensor'}, dimensions={1}, use_global_device_ids=true | all-gather | bytes 835584 | tf_op jit(solution)/shard_map/while/body/eval_jaxpr/all_gather | solution.py:107
  399.8 3.2 conditional.7
  399.8 3.2 fusion.16
  403.0 1.3 collective-permute-start
  404.3 10.4 %collective-permute-done = bf16[64,384]{1,0:T(8,128)(2,1)S(1)} collective-permute-done((bf16[64,384]{1,0:T(8,128)(2,1)S(1)}, bf16[64,384]{1,0:T(8,128)(2,1)S(1)}, u32[]{:S(2)}, u32[]{:S(2)}) %collective-permute-start) | collective-permute-done | bytes 49184 | tf_op jit(solution)/shard_map/while/body/eval_jaxpr/ppermute | solution.py:14
  414.8 0.8 dynamic-slice_select_fusion.2
  415.6 18.5 %all_gather.28 = bf16[64,6144]{1,0:T(8,128)(2,1)S(1)} all-gather(bf16[64,384]{1,0:T(8,128)(2,1)S(1)} %dynamic-slice_select_fusion.2), channel_id=1, replica_groups=mesh['section'=2,'tensor'=16,'dp'=8] {'tensor'}, dimensions={1}, use_global_device_ids=true | all-gather | bytes 835584 | tf_op jit(solution)/shard_map/while/body/eval_jaxpr/all_gather | solution.py:103
  434.1 10.5 %conditional.6 = (bf16[64,384]{1,0:T(8,128)(2,1)S(1)}, bf16[256,384]{0,1:T(8,128)(2,1)S(1)}, bf16[256,384]{0,1:T(8,128)(2,1)S(1)}) conditional(s32[]{:T(128)} %convert_element_type.61, (bf16[256,384]{0,1:T(8,128)(2,1)S(1)}, bf16[256,384]{0,1:T(8,128)(2,1)S(1)}) %tuple.64, (bf16[64,6144]{1,0:T(8,128)(2,1)S(1)}, bf16[6144,1152]{1,0:T(8,128)(2,1)}, ...), branch_computations={%region_3.3_spmd, %region_4.8_spmd} | conditional | flops 935560000 | bytes 18865236 | solution.py:104
  434.7 7.6 %convolution_convert_fusion = bf16[64,1152]{1,0:T(8,128)(2,1)S(1)} fusion(bf16[6144,1152]{1,0:T(8,128)(2,1)} %get-tuple-element.267, bf16[64,6144]{1,0:T(8,128)(2,1)S(1)} %get-tuple-element.266, f32[64]{0:T(128)S(1)} %add_rsqrt_fusion, f32[64]{0:T(128)S(1)} %broadcast_multiply_fusion), kind=kOutput, calls=%fused_computation.2 | convolution fusion | flops 907616256 | bytes 15090176 | tf_op jit(solution)/shard_map/while/body/eval_jaxpr/cond/branch_1_fun/dot_general | solution.py:50
  444.6 18.0 %all_gather.29 = bf16[64,6144]{1,0:T(8,128)(2,1)S(1)} all-gather(bf16[64,384]{1,0:T(8,128)(2,1)S(1)} %get-tuple-element.437), channel_id=1, replica_groups=mesh['section'=2,'tensor'=16,'dp'=8] {'tensor'}, dimensions={1}, use_global_device_ids=true | all-gather | bytes 835584 | tf_op jit(solution)/shard_map/while/body/eval_jaxpr/all_gather | solution.py:107
  462.5 3.2 conditional.7
  462.5 3.2 fusion.16
  465.7 1.3 collective-permute-start
  467.1 11.7 %collective-permute-done = bf16[64,384]{1,0:T(8,128)(2,1)S(1)} collective-permute-done((bf16[64,384]{1,0:T(8,128)(2,1)S(1)}, bf16[64,384]{1,0:T(8,128)(2,1)S(1)}, u32[]{:S(2)}, u32[]{:S(2)}) %collective-permute-start) | collective-permute-done | bytes 49184 | tf_op jit(solution)/shard_map/while/body/eval_jaxpr/ppermute | solution.py:14
  478.8 0.8 dynamic-slice_select_fusion.2
  479.6 18.2 %all_gather.28 = bf16[64,6144]{1,0:T(8,128)(2,1)S(1)} all-gather(bf16[64,384]{1,0:T(8,128)(2,1)S(1)} %dynamic-slice_select_fusion.2), channel_id=1, replica_groups=mesh['section'=2,'tensor'=16,'dp'=8] {'tensor'}, dimensions={1}, use_global_device_ids=true | all-gather | bytes 835584 | tf_op jit(solution)/shard_map/while/body/eval_jaxpr/all_gather | solution.py:103
  497.8 11.2 %conditional.6 = (bf16[64,384]{1,0:T(8,128)(2,1)S(1)}, bf16[256,384]{0,1:T(8,128)(2,1)S(1)}, bf16[256,384]{0,1:T(8,128)(2,1)S(1)}) conditional(s32[]{:T(128)} %convert_element_type.61, (bf16[256,384]{0,1:T(8,128)(2,1)S(1)}, bf16[256,384]{0,1:T(8,128)(2,1)S(1)}) %tuple.64, (bf16[64,6144]{1,0:T(8,128)(2,1)S(1)}, bf16[6144,1152]{1,0:T(8,128)(2,1)}, ...), branch_computations={%region_3.3_spmd, %region_4.8_spmd} | conditional | flops 935560000 | bytes 18865236 | solution.py:104
  498.5 7.6 %convolution_convert_fusion = bf16[64,1152]{1,0:T(8,128)(2,1)S(1)} fusion(bf16[6144,1152]{1,0:T(8,128)(2,1)} %get-tuple-element.267, bf16[64,6144]{1,0:T(8,128)(2,1)S(1)} %get-tuple-element.266, f32[64]{0:T(128)S(1)} %add_rsqrt_fusion, f32[64]{0:T(128)S(1)} %broadcast_multiply_fusion), kind=kOutput, calls=%fused_computation.2 | convolution fusion | flops 907616256 | bytes 15090176 | tf_op jit(solution)/shard_map/while/body/eval_jaxpr/cond/branch_1_fun/dot_general | solution.py:50
  506.5 0.7 dynamic_update_slice.7
  509.0 19.5 %all_gather.29 = bf16[64,6144]{1,0:T(8,128)(2,1)S(1)} all-gather(bf16[64,384]{1,0:T(8,128)(2,1)S(1)} %get-tuple-element.437), channel_id=1, replica_groups=mesh['section'=2,'tensor'=16,'dp'=8] {'tensor'}, dimensions={1}, use_global_device_ids=true | all-gather | bytes 835584 | tf_op jit(solution)/shard_map/while/body/eval_jaxpr/all_gather | solution.py:107
  528.5 3.2 conditional.7
  528.5 3.2 fusion.16
  531.7 1.3 collective-permute-start
  533.1 1.8 collective-permute-done
  (91 shorter events, 12.5 us)
Async XLA Ops:
  6.5 1.5 copy-start.1
  6.5 66.2 %all-gather.7.cloned.1.call-start = ((), (), s32[]{:S(2)}) async-start(), calls=%async_computation.1 | async-start | bytes 5308416 | tf_op jit(solution)/shard_map/all_gather | solution.py:33
  7.3 214.1 %all-gather.5.cloned.1.call-start = ((), (), s32[]{:S(2)}) async-start(), calls=%async_computation | async-start | bytes 15925248 | tf_op jit(solution)/shard_map/all_gather | solution.py:32
  260.7 26.8 %collective-permute-start = (bf16[64,384]{1,0:T(8,128)(2,1)S(1)}, bf16[64,384]{1,0:T(8,128)(2,1)S(1)}, u32[]{:S(2)}, u32[]{:S(2)}) collective-permute-start(bf16[64,384]{1,0:T(8,128)(2,1)S(1)} %get-tuple-element.497), channel_id=1, source_target_pairs={{0,128},{1,129},{2,130},{3,131},{4,132},{5,133},{6,134},{7,135},{8... | collective-permute-start | bytes 147464 | tf_op jit(solution)/shard_map/while/body/eval_jaxpr/ppermute | solution.py:14
  338.8 12.7 %collective-permute-start = (bf16[64,384]{1,0:T(8,128)(2,1)S(1)}, bf16[64,384]{1,0:T(8,128)(2,1)S(1)}, u32[]{:S(2)}, u32[]{:S(2)}) collective-permute-start(bf16[64,384]{1,0:T(8,128)(2,1)S(1)} %get-tuple-element.497), channel_id=1, source_target_pairs={{0,128},{1,129},{2,130},{3,131},{4,132},{5,133},{6,134},{7,135},{8... | collective-permute-start | bytes 147464 | tf_op jit(solution)/shard_map/while/body/eval_jaxpr/ppermute | solution.py:14
  403.0 11.8 %collective-permute-start = (bf16[64,384]{1,0:T(8,128)(2,1)S(1)}, bf16[64,384]{1,0:T(8,128)(2,1)S(1)}, u32[]{:S(2)}, u32[]{:S(2)}) collective-permute-start(bf16[64,384]{1,0:T(8,128)(2,1)S(1)} %get-tuple-element.497), channel_id=1, source_target_pairs={{0,128},{1,129},{2,130},{3,131},{4,132},{5,133},{6,134},{7,135},{8... | collective-permute-start | bytes 147464 | tf_op jit(solution)/shard_map/while/body/eval_jaxpr/ppermute | solution.py:14
  465.7 13.1 %collective-permute-start = (bf16[64,384]{1,0:T(8,128)(2,1)S(1)}, bf16[64,384]{1,0:T(8,128)(2,1)S(1)}, u32[]{:S(2)}, u32[]{:S(2)}) collective-permute-start(bf16[64,384]{1,0:T(8,128)(2,1)S(1)} %get-tuple-element.497), channel_id=1, source_target_pairs={{0,128},{1,129},{2,130},{3,131},{4,132},{5,133},{6,134},{7,135},{8... | collective-permute-start | bytes 147464 | tf_op jit(solution)/shard_map/while/body/eval_jaxpr/ppermute | solution.py:14
  531.7 3.1 collective-permute-start
  534.9 0.7 copy-start
Sparse Core Ops, SparseCore 0:
  9.1 63.5 all-gather.6
  74.5 146.7 all-gather.4
where the time goes:
time: 543 us; the launch traced here: 542 us
  waiting for transfers between devices  275 us (51%)
  blocking collectives  185 us (34%)
  matrix products  45.5 us (8%)
  between operations  13.4 us (2%)
  other arithmetic  8.09 us (1%)
  local copies, waits for them, and re-layouts  7.73 us (1%)
  starting transfers between devices  6.5 us (1%)
    all_gather x1, waiting for transfers between devices, local(): lax.all_gather(w_qkv[0], 'dp', axis=0, tiled=True)  149 us
    all_gather x5, blocking collectives, advance(): all_heads = lax.all_gather(head_out, 'tensor', axis=1, tiled=True)  93 us
    all_gather x5, blocking collectives, advance(): whole = lax.all_gather(current, 'tensor', axis=1, tiled=True)  92.4 us
    all_gather x1, waiting for transfers between devices, local(): lax.all_gather(w_out[0], 'dp', axis=0, tiled=True)  64.4 us
    ppermute x5, waiting for transfers between devices, shifted(): return lax.ppermute(array, axis, pairs)  60.7 us
    dot_general x4, matrix products, attention(): jnp.dot(normed, qkv_full, preferred_element_type=jnp.float32)  30.5 us
    dot_general x4, matrix products, project_out(): update = jnp.dot(all_heads, out_full, preferred_element_type=jnp.float32)  12.8 us
  transfers between devices with their start and end apart: 7, of which 7 were waited for; matrix products, arithmetic and copies ran while one was open for 0% of the time, Pallas kernels for 0%

commit v1 on v0

v1 whole, which is shorter than its diff:
```python
import functools
import math

import jax
import jax.numpy as jnp
from jax import lax
from jax.experimental import pallas as pl
from jax.experimental.pallas import tpu as pltpu
from jax.sharding import PartitionSpec as P

MESH = pl.DeviceIdType.MESH
HD = 128
HEADS = 3
LEN = 256
FEAT = 384
ROWS = 768
COLS = 1152
WIDTH = 6144
NZ = 8
GROUPS = ((0, 1), (1, 2), (3, 2), (5, 2), (7, 1))
F32 = jnp.float32
BF16 = jnp.bfloat16


def kernel(
    doc_ref, hid_ref, wq_hbm, wo_hbm, out_ref,
    xin, xc, wq, wo, stat, csum, trans, mask, proj, att, res,
    xbuf, abuf, part, send3, recv3, part6, send6, recv6,
    load_sem, hand_sem,
    s1s, s1r, s4s, s4r, a2s, a2r, b2s, b2r, a5s, a5r, b5s, b5r,
    sts, str_, css, csr, s3s, s3r, s6s, s6r,
):
    s = lax.axis_index("section")
    t = lax.axis_index("tensor")
    z = lax.axis_index("dp")
    y, x = t // 4, t % 4
    plane = t // 2
    half = t % 2
    at_home = plane == z

    def along_z(by):
        return (s, t, (z + by + NZ) % NZ)

    def in_plane(dy, dx):
        return (s, ((y + dy) % 4) * 4 + (x + dx) % 4, z)

    def copy(src, dst, send_sem, recv_sem, device):
        return pltpu.make_async_remote_copy(
            src_ref=src, dst_ref=dst, send_sem=send_sem, recv_sem=recv_sem,
            device_id=device, device_id_type=MESH,
        )

    load_q = pltpu.make_async_copy(wq_hbm.at[0], wq, load_sem.at[0])
    load_o = pltpu.make_async_copy(wo_hbm.at[0], wo, load_sem.at[1])
    load_x = pltpu.make_async_copy(hid_ref.at[0], xin, load_sem.at[2])

    @pl.when(s == 0)
    def _():
        load_x.start()

    load_q.start()
    load_o.start()

    barrier = pltpu.get_barrier_semaphore()

    def greet(device):
        pl.semaphore_signal(barrier, inc=1, device_id=device, device_id_type=MESH)

    def greet_source(i, c):
        source_t, source_z = 2 * z + i % 2, i // 2

        @pl.when(jnp.logical_not((source_t == t) & (source_z == z)))
        def _():
            greet((s, source_t, source_z))

        return c

    lax.fori_loop(0, 16, greet_source, 0)

    def greet_plane(i, c):
        greet(in_plane(i // 4, i % 4))
        return c

    lax.fori_loop(1, 16, greet_plane, 0)

    def greet_line(i, c):
        greet(along_z(i))
        return c

    lax.fori_loop(1, NZ, greet_line, 0)
    greet((1 - s, t, z))
    pl.semaphore_wait(barrier, 16 + 15 + 7 + 1 - at_home.astype(jnp.int32))

    hand = copy(res, xin, hand_sem.at[0], hand_sem.at[1], (1 - s, t, z))

    @pl.when(s == 0)
    def _():
        load_x.wait()

    @pl.when(s == 1)
    def _():
        hand.wait_recv()

    xf = xin[...].astype(F32)
    own_mean = jnp.mean(xf, axis=1, keepdims=True)
    centred = xf - own_mean
    own_sq = jnp.sum(centred * centred, axis=1, keepdims=True)
    xc[...] = centred.astype(BF16)

    rel = (z - plane + NZ) % NZ
    slot = jnp.where(rel < 4, 7 - 2 * rel, 2 * rel - 8)

    def spread_copy(src, buf, ssem, rsem, g):
        rows = pl.ds(pl.multiple_of(g * 16, 16), 16)
        there = pl.ds(pl.multiple_of((g % 4) * 16, 16), 16)
        cols = pl.ds(pl.multiple_of(half * FEAT, 128), FEAT)
        from_ref, to_ref = src.at[rows, :], buf.at[slot, g // 4, there, cols]

        def remote():
            return copy(from_ref, to_ref, ssem.at[g], rsem.at[slot, half], (s, g, plane))

        def local():
            return pltpu.make_async_copy(from_ref, to_ref, rsem.at[slot, half])

        return remote, local

    def spread(src, buf, ssem, rsem):
        def body(g, c):
            remote, local = spread_copy(src, buf, ssem, rsem, g)
            own = at_home & (g == t)

            @pl.when(own)
            def _():
                local().start()

            @pl.when(jnp.logical_not(own))
            def _():
                remote().start()

            return c

        lax.fori_loop(0, 16, body, 0)

    def spread_drain(src, buf, ssem, rsem):
        def body(g, c):
            remote, _ = spread_copy(src, buf, ssem, rsem, g)

            @pl.when(jnp.logical_not(at_home & (g == t)))
            def _():
                remote().wait_send()

            return c

        lax.fori_loop(0, 16, body, 0)

    def spread_wait(buf, rsem, k, h):
        there = buf.at[k, y, pl.ds(pl.multiple_of(x * 16, 16), 16), pl.ds(h * FEAT, FEAT)]
        pltpu.make_async_copy(there, there, rsem.at[k, h]).wait()

    def gather_copy(buf, sems, step, grp, h, j):
        k0, n = GROUPS[grp]
        own = pl.ds(pl.multiple_of(x * 16, 16), 16)
        cols = pl.ds(h * FEAT, FEAT)
        if step == 0:
            ref = buf.at[pl.ds(k0, n), y, own, cols]
        elif h == 0:
            ref = buf.at[pl.ds(k0, n), y, :, cols]
        else:
            ref = buf.at[pl.ds(k0, n), :, own, cols]
        device = in_plane(0, j) if (step == h) else in_plane(j, 0)
        return copy(ref, ref, sems[2 * step].at[grp, h, j - 1], sems[2 * step + 1].at[grp, h, j - 1], device)

    def gather_first(buf, sems, rsem, grp):
        k0, n = GROUPS[grp]
        for h in range(2):
            for k in range(k0, k0 + n):
                spread_wait(buf, rsem, k, h)
            for j in (2, 1, 3):
                gather_copy(buf, sems, 0, grp, h, j).start()

    def gather_second(buf, sems, grp):
        for h in range(2):
            for j in (1, 2, 3):
                gather_copy(buf, sems, 0, grp, h, j).wait_recv()
            for j in (2, 1, 3):
                gather_copy(buf, sems, 1, grp, h, j).start()

    def gather_last(buf, sems, grp):
        for h in range(2):
            for j in (1, 2, 3):
                gather_copy(buf, sems, 1, grp, h, j).wait_recv()

    def gather_drain(buf, sems):
        for grp in range(len(GROUPS)):
            for step in range(2):
                for h in range(2):
                    for j in (1, 2, 3):
                        gather_copy(buf, sems, step, grp, h, j).wait_send()

    spread(xc, xbuf, s1s, s1r)

    lane = lax.broadcasted_iota(jnp.int32, (LEN, 128), 1)
    columns = jnp.where(lane == 0, own_mean, jnp.where(lane == 1, own_sq, 0.0))
    stat[t] = jnp.transpose(columns)[0:8, :]

    def stat_copy(i):
        return copy(stat.at[t], stat.at[t], sts.at[i - 1], str_.at[i - 1], in_plane(i // 4, i % 4))

    def stat_send(i, c):
        stat_copy(i).start()
        return c

    lax.fori_loop(1, 16, stat_send, 0)

    load_q.wait()
    row16 = lax.broadcasted_iota(jnp.int32, (16, ROWS), 0)
    col16 = lax.broadcasted_iota(jnp.int32, (16, ROWS), 1)
    pick = jnp.where(row16 == col16 // FEAT, 1.0, 0.0).astype(BF16)
    csum[z] = jnp.dot(pick, wq[...], preferred_element_type=F32)[0:8, :]
    csum[NZ : 2 * NZ] = jnp.zeros((NZ, 8, COLS), F32)

    def csum_copy(i):
        return copy(csum.at[z], csum.at[z], css.at[i - 1], csr.at[i - 1], along_z(i))

    def csum_send(i, c):
        csum_copy(i).start()
        return c

    lax.fori_loop(1, NZ, csum_send, 0)

    sems2 = (a2s, a2r, b2s, b2r)
    sems5 = (a5s, a5r, b5s, b5r)

    def product(buf, k, w, into, tiles):
        rows = buf[k].reshape(LEN, ROWS)

        def body(n, c):
            cols = pl.ds(pl.multiple_of(n * FEAT, 128), FEAT)
            into[k, :, cols] = jnp.dot(rows, w[:, cols], preferred_element_type=F32)
            return c

        lax.fori_loop(0, tiles, body, 0)

    def ring_copy(k, q):
        rows = pl.ds(q * 64, 64)
        up = q < 2 if k == 0 else k % 2 == 1
        return copy(send3.at[k, rows], recv3.at[k, rows], s3s.at[k, q], s3r.at[k, q], along_z(1 if up else -1))

    def ring_step(k, q, before):
        rows = pl.ds(q * 64, 64)
        value = part[k, rows, :]
        if before is not None:
            ring_copy(before, q).wait_recv()
            value = value + recv3[before, rows, :].astype(F32)
        send3[k, rows, :] = value.astype(BF16)
        ring_copy(k, q).start()

    for grp in range(5):
        gather_first(xbuf, sems2, s1r, grp)

    row_pos = lax.broadcasted_iota(jnp.int32, (LEN, LEN), 0)
    col_pos = lax.broadcasted_iota(jnp.int32, (LEN, LEN), 1)
    row_doc = jnp.zeros((LEN, LEN), jnp.int32)
    col_doc = jnp.zeros((LEN, LEN), jnp.int32)
    end = jnp.int32(0)
    for i in range(4):
        end = end + doc_ref[0, i]
        row_doc = row_doc + (row_pos >= end).astype(jnp.int32)
        col_doc = col_doc + (col_pos >= end).astype(jnp.int32)
    mask[...] = jnp.where((col_pos <= row_pos) & (row_doc == col_doc), 1.0, 0.0)

    gather_second(xbuf, sems2, 0)
    gather_second(xbuf, sems2, 1)
    gather_last(xbuf, sems2, 0)
    product(xbuf, 0, wq, part, 3)
    for q in (0, 2, 1, 3):
        ring_step(0, q, None)
    gather_second(xbuf, sems2, 2)
    gather_last(xbuf, sems2, 1)
    product(xbuf, 1, wq, part, 3)
    ring_step(1, 2, None)
    ring_step(1, 3, None)
    product(xbuf, 2, wq, part, 3)
    ring_step(2, 0, None)
    ring_step(2, 1, None)
    gather_second(xbuf, sems2, 3)
    gather_last(xbuf, sems2, 2)
    product(xbuf, 3, wq, part, 3)
    product(xbuf, 4, wq, part, 3)
    ring_step(1, 0, 0)
    ring_step(2, 2, 0)
    ring_step(1, 1, 0)
    ring_step(2, 3, 0)
    gather_second(xbuf, sems2, 4)
    gather_last(xbuf, sems2, 3)
    product(xbuf, 5, wq, part, 3)
    product(xbuf, 6, wq, part, 3)
    up_order, down_order = (2, 3, 0, 1), (0, 1, 2, 3)
    for i in range(4):
        ring_step(3, up_order[i], 1)
        ring_step(4, down_order[i], 2)
    gather_last(xbuf, sems2, 4)
    product(xbuf, 7, wq, part, 3)
    for i in range(4):
        ring_step(5, up_order[i], 3)
        ring_step(6, down_order[i], 4)

    for i in range(1, 16):
        stat_copy(i).wait_recv()
    means = [stat[i, 0:1, :] for i in range(16)]
    mean = functools.reduce(lambda a, b: a + b, means) * (1.0 / 16)
    square = functools.reduce(lambda a, b: a + b, [stat[i, 1:2, :] for i in range(16)])
    trans[...] = jnp.zeros((128, LEN), F32)
    for i in range(16):
        off = means[i] - mean
        square = square + FEAT * (off * off)
        trans[pl.ds((i // 2) * 8 + i % 2, 1), :] = off
    trans[pl.ds(64, 1), :] = lax.rsqrt(square * (1.0 / WIDTH) + 1e-05)
    turned = jnp.transpose(trans[...])
    scale = turned[:, 64:65]
    m_high = turned.astype(BF16)
    m_low = (turned - m_high.astype(F32)).astype(BF16)
    for i in range(1, NZ):
        csum_copy(i).wait_recv()
    sums = csum[...].reshape(128, COLS)
    c_high = sums.astype(BF16)
    c_low = (sums - c_high.astype(F32)).astype(BF16)
    part[7] = part[7] + (
        jnp.dot(m_high, c_high, preferred_element_type=F32)
        + jnp.dot(m_low, c_high, preferred_element_type=F32)
        + jnp.dot(m_high, c_low, preferred_element_type=F32)
    )

    for q in range(4):
        rows = pl.ds(q * 64, 64)
        ring_copy(5, q).wait_recv()
        ring_copy(6, q).wait_recv()
        total = part[7, rows, :] + recv3[5, rows, :].astype(F32) + recv3[6, rows, :].astype(F32)
        proj[rows, :] = (total * scale[q * 64 : q * 64 + 64, :]).astype(BF16)

    allowed = mask[...] > 0.5
    for head in range(HEADS):
        base = head * 3 * HD
        query = proj[:, base : base + HD]
        keys = proj[:, base + HD : base + 2 * HD]
        values = proj[:, base + 2 * HD : base + 3 * HD]
        scores = lax.dot_general(query, keys, (((1,), (1,)), ((), ())), preferred_element_type=F32)
        scores = jnp.where(allowed, scores * (1.0 / math.sqrt(HD)), -1e30)
        weights = jnp.exp(scores - jnp.max(scores, axis=1, keepdims=True))
        soft = (weights / jnp.sum(weights, axis=1, keepdims=True)).astype(BF16)
        att[:, head * HD : (head + 1) * HD] = jnp.dot(soft, values, preferred_element_type=F32).astype(BF16)

    spread(att, abuf, s4s, s4r)
    load_o.wait()

    def sum_copy(k, part_of=0):
        if k == 0:
            rows = pl.ds(part_of * 128, 128)
            return copy(send6.at[0, rows], recv6.at[0, rows], s6s.at[0, part_of], s6r.at[0, part_of], along_z(-2 if part_of else 2))
        by = {1: 1, 2: -1, 3: 2, 4: -2, 5: 1, 6: -1}[k]
        return copy(send6.at[k], recv6.at[k], s6s.at[k, 0], s6r.at[k, 0], along_z(by))

    for grp in range(5):
        gather_first(abuf, sems5, s4r, grp)
    gather_second(abuf, sems5, 0)
    gather_second(abuf, sems5, 1)
    gather_last(abuf, sems5, 0)
    product(abuf, 0, wo, part6, 1)
    send6[0] = part6[0].astype(BF16)
    sum_copy(0, 0).start()
    sum_copy(0, 1).start()
    gather_second(abuf, sems5, 2)
    gather_last(abuf, sems5, 1)
    for k in (1, 2):
        product(abuf, k, wo, part6, 1)
        send6[k] = part6[k].astype(BF16)
        sum_copy(k).start()
    gather_second(abuf, sems5, 3)
    gather_last(abuf, sems5, 2)
    for k in (3, 4):
        product(abuf, k, wo, part6, 1)
    gather_second(abuf, sems5, 4)
    gather_last(abuf, sems5, 3)
    for k in (5, 6):
        product(abuf, k, wo, part6, 1)
        send6[k] = part6[k].astype(BF16)
        sum_copy(k).start()
    for k in (3, 4):
        sum_copy(0, k - 3).wait_recv()
        sum_copy(k - 2).wait_recv()
        total = part6[k] + recv6[k - 2].astype(F32)
        send6[k] = total.astype(BF16)
        rows = pl.ds((k - 3) * 128, 128)
        both = part6[k, rows, :] + recv6[k - 2, rows, :].astype(F32) + recv6[0, rows, :].astype(F32)
        send6[k, rows, :] = both.astype(BF16)
        sum_copy(k).start()
    gather_last(abuf, sems5, 4)
    product(abuf, 7, wo, part6, 1)
    total = part6[7] + xin[...].astype(F32)
    for k in (5, 6, 3, 4):
        sum_copy(k).wait_recv()
        total = total + recv6[k].astype(F32)
    result = total.astype(BF16)
    res[...] = result

    @pl.when(s == 0)
    def _():
        hand.start()

    out_ref[0, 0] = result

    spread_drain(xc, xbuf, s1s, s1r)
    spread_drain(att, abuf, s4s, s4r)
    gather_drain(xbuf, sems2)
    gather_drain(abuf, sems5)

    def stat_drain(i, c):
        stat_copy(i).wait_send()
        return c

    lax.fori_loop(1, 16, stat_drain, 0)

    def csum_drain(i, c):
        csum_copy(i).wait_send()
        return c

    lax.fori_loop(1, NZ, csum_drain, 0)
    for k in range(7):
        for q in range(4):
            ring_copy(k, q).wait_send()
    sum_copy(0, 0).wait_send()
    sum_copy(0, 1).wait_send()
    for k in range(1, 7):
        sum_copy(k).wait_send()

    @pl.when(s == 0)
    def _():
        hand.wait_send()


def local(hidden_in, doc_lengths, w_qkv, w_out):
    vmem, dma = pltpu.VMEM, pltpu.SemaphoreType.DMA
    return pl.pallas_call(
        kernel,
        out_shape=jax.ShapeDtypeStruct((1, 1, LEN, FEAT), BF16),
        in_specs=[
            pl.BlockSpec(memory_space=pltpu.SMEM),
            pl.BlockSpec(memory_space=pl.ANY),
            pl.BlockSpec(memory_space=pl.ANY),
            pl.BlockSpec(memory_space=pl.ANY),
        ],
        out_specs=pl.BlockSpec(memory_space=pltpu.VMEM),
        scratch_shapes=[
            vmem((LEN, FEAT), BF16),
            vmem((LEN, FEAT), BF16),
            vmem((ROWS, COLS), BF16),
            vmem((ROWS, FEAT), BF16),
            vmem((16, 8, LEN), F32),
            vmem((16, 8, COLS), F32),
            vmem((128, LEN), F32),
            vmem((LEN, LEN), F32),
            vmem((LEN, COLS), BF16),
            vmem((LEN, FEAT), BF16),
            vmem((LEN, FEAT), BF16),
            vmem((8, 4, 64, ROWS), BF16),
            vmem((8, 4, 64, ROWS), BF16),
            vmem((8, LEN, COLS), F32),
            vmem((7, LEN, COLS), BF16),
            vmem((7, LEN, COLS), BF16),
            vmem((8, LEN, FEAT), F32),
            vmem((7, LEN, FEAT), BF16),
            vmem((7, LEN, FEAT), BF16),
            dma((3,)), dma((2,)),
            dma((16,)), dma((8, 2)), dma((16,)), dma((8, 2)),
            dma((5, 2, 3)), dma((5, 2, 3)), dma((5, 2, 3)), dma((5, 2, 3)),
            dma((5, 2, 3)), dma((5, 2, 3)), dma((5, 2, 3)), dma((5, 2, 3)),
            dma((15,)), dma((15,)), dma((7,)), dma((7,)),
            dma((7, 4)), dma((7, 4)), dma((7, 2)), dma((7, 2)),
        ],
        compiler_params=pltpu.CompilerParams(
            collective_id=0, has_side_effects=True, vmem_limit_bytes=56 * 1024 * 1024
        ),
        cost_estimate=pl.CostEstimate(
            flops=2 * 2048 * ROWS * (COLS + FEAT), bytes_accessed=3 * 1024 * 1024, transcendentals=3 * LEN * LEN
        ),
    )(doc_lengths, hidden_in, w_qkv, w_out)


def solution(mesh):
    return jax.shard_map(
        local,
        mesh=mesh,
        in_specs=(
            P("dp", None, "tensor"),
            P("dp", None),
            P("section", "dp", "tensor"),
            P("section", "dp", "tensor"),
        ),
        out_specs=P("section", "dp", None, "tensor"),
        check_vma=False,
    )
```

time: 543 us -> 183 us (0.34)
  waiting for transfers between devices: 275 us -> 0 us
  blocking collectives: 185 us -> 0 us
  Pallas kernels: 0 us -> 181 us
  matrix products: 45.5 us -> 0 us
  between operations: 13.4 us -> 0.01 us
  other arithmetic: 8.09 us -> 0 us
  starting transfers between devices: 6.5 us -> 0 us
  local copies, waits for them, and re-layouts: 7.73 us -> 1.62 us
    all_gather x2 -> x0, waiting for transfers between devices: 213 us -> none  [the longest x1 149 us: local(): lax.all_gather(w_qkv[0], 'dp', axis=0, tiled=True)]
    all_gather x10 -> x0, blocking collectives: 185 us -> none  [the longest x5 93 us: advance(): all_heads = lax.all_gather(head_out, 'tensor', axis=1, tiled=True)]
    pallas_call x0 -> x1, Pallas kernels: none -> 181 us  [local(): pl.pallas_call(kernel, out_shape=jax.ShapeDtypeStruct((1, 1, LEN, FEAT),...]
    ppermute x5 -> x0, waiting for transfers between devices: 60.7 us -> none  [shifted(): return lax.ppermute(array, axis, pairs)]
    dot_general x16 -> x0, matrix products: 45.5 us -> none  [the longest x4 30.5 us: attention(): jnp.dot(normed, qkv_full, preferred_element_type=jnp.float32)]
    ppermute x5 -> x0, starting transfers between devices: 6.45 us -> none  [shifted(): return lax.ppermute(array, axis, pairs)]
  transfers between devices with their start and end apart: 7 -> 0, of which waited for: 7 -> 0; matrix products, arithmetic and copies ran while one was open for 0% -> 0% of each run, Pallas kernels for 0% -> 0%
where the time goes in v1:
time: 183 us; the launch traced here: 182 us
  Pallas kernels  181 us (99%)
    pallas_call x1, Pallas kernels, local(): pl.pallas_call(kernel, out_shape=jax.ShapeDtypeStruct((1, 1, LEN, FEAT),...  181 us

profile of v1, /device:TPU:1, one launch (start us, length us, event | category | flops | bytes accessed | tf_op | source)
XLA Modules:
  0.0 182.5 jit_solution(8852924522575362334)
XLA Ops:
  0.0 180.8 %shard_map.46 = bf16[1,1,256,384]{3,2,1,0:T(8,128)(2,1)} custom-call(s32[1,4]{1,0:T(1,128)} %doc_ref.1, bf16[1,256,384]{2,1,0:T(8,128)(2,1)} %hid_ref.1, bf16[1,768,1152]{2,1,0:T(8,128)(2,1)} %wq_hbm.1, bf16[1,768,384]{2,1,0:T(8,128)(2,1)} %wo_hbm.1), custom_call_target="tpu_custom_call" | custom-call | flops 4831838208 | bytes 3145728 | tf_op jit(solution)/shard_map/pallas_call | solution.py:443
  180.9 1.6 copy.6

commit v2 on v1

--- a/solution.py
+++ b/solution.py
@@ -24,11 +24,11 @@
 
 def kernel(
     doc_ref, hid_ref, wq_hbm, wo_hbm, out_ref,
-    xin, xc, wq, wo, stat, csum, trans, mask, proj, att, res,
-    xbuf, abuf, part, send3, recv3, part6, send6, recv6,
-    load_sem, hand_sem,
-    s1s, s1r, s4s, s4r, a2s, a2r, b2s, b2r, a5s, a5r, b5s, b5r,
-    sts, str_, css, csr, s3s, s3r, s6s, s6r,
+    xin, xc, xc2, wq, wo, stat, stat2, csum, trans, mask, proj, res,
+    xbuf, abuf, part, send3, recv3,
+    load_sem, hand_sem, go_sem,
+    s1s, s1r, a2s, a2r, b2s, b2r, d2s, d2r, a5s, a5r, b5s, b5r,
+    t1s, sts, str_, st2s, css, csr, s3s, s3r, wos, wor,
 ):
     s = lax.axis_index("section")
     t = lax.axis_index("tensor")
@@ -37,6 +37,10 @@
     plane = t // 2
     half = t % 2
     at_home = plane == z
+    rel = (z - plane + NZ) % NZ
+    slot = jnp.where(rel < 4, 7 - 2 * rel, 2 * rel - 8)
+    far = (rel >= 3) & (rel <= 5)
+    first = s == 0
 
     def along_z(by):
         return (s, t, (z + by + NZ) % NZ)
@@ -51,7 +55,7 @@
         )
 
     load_q = pltpu.make_async_copy(wq_hbm.at[0], wq, load_sem.at[0])
-    load_o = pltpu.make_async_copy(wo_hbm.at[0], wo, load_sem.at[1])
+    load_o = pltpu.make_async_copy(wo_hbm.at[0], wo.at[z], load_sem.at[1])
     load_x = pltpu.make_async_copy(hid_ref.at[0], xin, load_sem.at[2])
 
     @pl.when(s == 0)
@@ -69,9 +73,9 @@
     def greet_source(i, c):
         source_t, source_z = 2 * z + i % 2, i // 2
 
-        @pl.when(jnp.logical_not((source_t == t) & (source_z == z)))
+        @pl.when(jnp.logical_not(first & (source_t == t) & (source_z == z)))
         def _():
-            greet((s, source_t, source_z))
+            greet((0, source_t, source_z))
 
         return c
 
@@ -88,45 +92,84 @@
         return c
 
     lax.fori_loop(1, NZ, greet_line, 0)
-    greet((1 - s, t, z))
-    pl.semaphore_wait(barrier, 16 + 15 + 7 + 1 - at_home.astype(jnp.int32))
-
-    hand = copy(res, xin, hand_sem.at[0], hand_sem.at[1], (1 - s, t, z))
-
-    @pl.when(s == 0)
+
+    @pl.when(s == 1)
+    def _():
+        def greet_before(i, c):
+            greet((0, i, z))
+            return c
+
+        lax.fori_loop(0, 16, greet_before, 0)
+
+    load_q.wait()
+    row16 = lax.broadcasted_iota(jnp.int32, (16, ROWS), 0)
+    col16 = lax.broadcasted_iota(jnp.int32, (16, ROWS), 1)
+    pick = jnp.where(row16 == col16 // FEAT, 1.0, 0.0).astype(BF16)
+    csum[z] = jnp.dot(pick, wq[...], preferred_element_type=F32)[0:8, :]
+    csum[NZ : 2 * NZ] = jnp.zeros((NZ, 8, COLS), F32)
+
+    def csum_copy(i):
+        return copy(csum.at[z], csum.at[z], css.at[i - 1], csr.at[i - 1], along_z(i))
+
+    def csum_send(i, c):
+        csum_copy(i).start()
+        return c
+
+    def centre(value):
+        own_mean = jnp.mean(value, axis=1, keepdims=True)
+        off = value - own_mean
+        own_sq = jnp.sum(off * off, axis=1, keepdims=True)
+        lane = lax.broadcasted_iota(jnp.int32, (LEN, 128), 1)
+        columns = jnp.where(lane == 0, own_mean, jnp.where(lane == 1, own_sq, 0.0))
+        return off.astype(BF16), jnp.transpose(columns)[0:8, :]
+
+    def stat_copy(i):
+        return copy(stat.at[t], stat.at[t], sts.at[i - 1], str_.at[i], in_plane(i // 4, i % 4))
+
+    def stat_send(i, c):
+        stat_copy(i).start()
+        return c
+
+    def stat_on_copy(i):
+        _, there, same_z = in_plane(i // 4, i % 4)
+        return copy(stat2, stat.at[t], st2s.at[i], str_.at[i], (1, there, same_z))
+
+    def stat_on_send(i, c):
+        stat_on_copy(i).start()
+        return c
+
+    def hand():
+        return copy(res, xin, hand_sem.at[0], hand_sem.at[1], (1, t, z))
+
+    @pl.when(first)
     def _():
         load_x.wait()
-
-    @pl.when(s == 1)
-    def _():
-        hand.wait_recv()
-
-    xf = xin[...].astype(F32)
-    own_mean = jnp.mean(xf, axis=1, keepdims=True)
-    centred = xf - own_mean
-    own_sq = jnp.sum(centred * centred, axis=1, keepdims=True)
-    xc[...] = centred.astype(BF16)
-
-    rel = (z - plane + NZ) % NZ
-    slot = jnp.where(rel < 4, 7 - 2 * rel, 2 * rel - 8)
-
-    def spread_copy(src, buf, ssem, rsem, g):
+        low, rows = centre(xin[...].astype(F32))
+        xc[...] = low
+        stat[t] = rows
+
+    pl.semaphore_wait(barrier, jnp.where(first, 16 + 16 + 16 - at_home.astype(jnp.int32), 0) + 15 + 7)
+
+    def spread_copy(src, buf, ssem, rsem, to, g):
         rows = pl.ds(pl.multiple_of(g * 16, 16), 16)
         there = pl.ds(pl.multiple_of((g % 4) * 16, 16), 16)
         cols = pl.ds(pl.multiple_of(half * FEAT, 128), FEAT)
         from_ref, to_ref = src.at[rows, :], buf.at[slot, g // 4, there, cols]
 
         def remote():
-            return copy(from_ref, to_ref, ssem.at[g], rsem.at[slot, half], (s, g, plane))
+            return copy(from_ref, to_ref, ssem.at[g], rsem.at[slot, half], (to, g, plane))
 
         def local():
             return pltpu.make_async_copy(from_ref, to_ref, rsem.at[slot, half])
 
         return remote, local
 
-    def spread(src, buf, ssem, rsem):
+    def spread(src, buf, ssem, rsem, to, other_core=False):
         def body(g, c):
-            remote, local = spread_copy(src, buf, ssem, rsem, g)
+            remote, local = spread_copy(src, buf, ssem, rsem, to, g)
+            if other_core:
+                remote().start()
+                return c
             own = at_home & (g == t)
 
             @pl.when(own)
@@ -141,9 +184,12 @@
 
         lax.fori_loop(0, 16, body, 0)
 
-    def spread_drain(src, buf, ssem, rsem):
+    def spread_drain(src, buf, ssem, rsem, to, other_core=False):
         def body(g, c):
-            remote, _ = spread_copy(src, buf, ssem, rsem, g)
+            remote, _ = spread_copy(src, buf, ssem, rsem, to, g)
+            if other_core:
+                remote().wait_send()
+                return c
 
             @pl.when(jnp.logical_not(at_home & (g == t)))
             def _():
@@ -170,6 +216,27 @@
         device = in_plane(0, j) if (step == h) else in_plane(j, 0)
         return copy(ref, ref, sems[2 * step].at[grp, h, j - 1], sems[2 * step + 1].at[grp, h, j - 1], device)
 
+    def direct_copy(buf, sems, i):
+        ref = buf.at[0, y, pl.ds(pl.multiple_of(x * 16, 16), 16), :]
+        return copy(ref, ref, sems[4].at[i - 1], sems[5].at[i - 1], in_plane(i // 4, i % 4))
+
+    def gather_direct(buf, sems, rsem):
+        spread_wait(buf, rsem, 0, 0)
+        spread_wait(buf, rsem, 0, 1)
+
+        def body(i, c):
+            direct_copy(buf, sems, 16 - i).start()
+            return c
+
+        lax.fori_loop(1, 16, body, 0)
+
+    def direct_wait(buf, sems):
+        def body(i, c):
+            direct_copy(buf, sems, i).wait_recv()
+            return c
+
+        lax.fori_loop(1, 16, body, 0)
+
     def gather_first(buf, sems, rsem, grp):
         k0, n = GROUPS[grp]
         for h in range(2):
@@ -191,45 +258,55 @@
                 gather_copy(buf, sems, 1, grp, h, j).wait_recv()
 
     def gather_drain(buf, sems):
-        for grp in range(len(GROUPS)):
+        def body(i, c):
+            direct_copy(buf, sems, i).wait_send()
+            return c
+
+        lax.fori_loop(1, 16, body, 0)
+        for grp in range(1, len(GROUPS)):
             for step in range(2):
                 for h in range(2):
                     for j in (1, 2, 3):
                         gather_copy(buf, sems, step, grp, h, j).wait_send()
 
-    spread(xc, xbuf, s1s, s1r)
-
-    lane = lax.broadcasted_iota(jnp.int32, (LEN, 128), 1)
-    columns = jnp.where(lane == 0, own_mean, jnp.where(lane == 1, own_sq, 0.0))
-    stat[t] = jnp.transpose(columns)[0:8, :]
-
-    def stat_copy(i):
-        return copy(stat.at[t], stat.at[t], sts.at[i - 1], str_.at[i - 1], in_plane(i // 4, i % 4))
-
-    def stat_send(i, c):
-        stat_copy(i).start()
-        return c
-
-    lax.fori_loop(1, 16, stat_send, 0)
-
-    load_q.wait()
-    row16 = lax.broadcasted_iota(jnp.int32, (16, ROWS), 0)
-    col16 = lax.broadcasted_iota(jnp.int32, (16, ROWS), 1)
-    pick = jnp.where(row16 == col16 // FEAT, 1.0, 0.0).astype(BF16)
-    csum[z] = jnp.dot(pick, wq[...], preferred_element_type=F32)[0:8, :]
-    csum[NZ : 2 * NZ] = jnp.zeros((NZ, 8, COLS), F32)
-
-    def csum_copy(i):
-        return copy(csum.at[z], csum.at[z], css.at[i - 1], csr.at[i - 1], along_z(i))
-
-    def csum_send(i, c):
-        csum_copy(i).start()
-        return c
+    @pl.when(first & far)
+    def _():
+        spread(xc, xbuf, s1s, s1r, 0)
+
+    @pl.when(first)
+    def _():
+        lax.fori_loop(1, 16, stat_send, 0)
 
     lax.fori_loop(1, NZ, csum_send, 0)
 
-    sems2 = (a2s, a2r, b2s, b2r)
-    sems5 = (a5s, a5r, b5s, b5r)
+    @pl.when(first & jnp.logical_not(far))
+    def _():
+        spread(xc, xbuf, s1s, s1r, 0)
+
+    sems2 = (a2s, a2r, b2s, b2r, d2s, d2r)
+
+    def weight_copy(step, way):
+        chunk = (z + (step if way else -step) + NZ) % NZ
+        if step == 3:
+            rows = pl.ds(FEAT if way else 0, FEAT)
+            ref = wo.at[chunk, rows]
+        else:
+            ref = wo.at[chunk]
+        return copy(ref, ref, wos.at[way, step], wor.at[way, step], along_z(-1 if way else 1))
+
+    def weight_step(step):
+        for way in range(2):
+            if step:
+                weight_copy(step - 1, way).wait_recv()
+            if step < 4:
+                weight_copy(step, way).start()
+
+    @pl.when(s == 1)
+    def _():
+        pl.semaphore_wait(go_sem, 1)
+
+    load_o.wait()
+    weight_step(0)
 
     def product(buf, k, w, into, tiles):
         rows = buf[k].reshape(LEN, ROWS)
@@ -255,8 +332,11 @@
         send3[k, rows, :] = value.astype(BF16)
         ring_copy(k, q).start()
 
-    for grp in range(5):
+    gather_direct(xbuf, sems2, s1r)
+    for grp in range(1, 5):
         gather_first(xbuf, sems2, s1r, grp)
+
+    weight_step(1)
 
     row_pos = lax.broadcasted_iota(jnp.int32, (LEN, LEN), 0)
     col_pos = lax.broadcasted_iota(jnp.int32, (LEN, LEN), 1)
@@ -269,9 +349,8 @@
         col_doc = col_doc + (col_pos >= end).astype(jnp.int32)
     mask[...] = jnp.where((col_pos <= row_pos) & (row_doc == col_doc), 1.0, 0.0)
 
-    gather_second(xbuf, sems2, 0)
     gather_second(xbuf, sems2, 1)
-    gather_last(xbuf, sems2, 0)
+    direct_wait(xbuf, sems2)
     product(xbuf, 0, wq, part, 3)
     for q in (0, 2, 1, 3):
         ring_step(0, q, None)
@@ -305,8 +384,17 @@
         ring_step(5, up_order[i], 3)
         ring_step(6, down_order[i], 4)
 
+    @pl.when(first)
+    def _():
+        pl.semaphore_signal(go_sem, inc=1, device_id=(1, t, z), device_id_type=MESH)
+
     for i in range(1, 16):
         stat_copy(i).wait_recv()
+
+    @pl.when(s == 1)
+    def _():
+        stat_on_copy(0).wait_recv()
+
     means = [stat[i, 0:1, :] for i in range(16)]
     mean = functools.reduce(lambda a, b: a + b, means) * (1.0 / 16)
     square = functools.reduce(lambda a, b: a + b, [stat[i, 1:2, :] for i in range(16)])
@@ -338,6 +426,21 @@
         total = part[7, rows, :] + recv3[5, rows, :].astype(F32) + recv3[6, rows, :].astype(F32)
         proj[rows, :] = (total * scale[q * 64 : q * 64 + 64, :]).astype(BF16)
 
+    weight_step(2)
+
+    def head_copy(step, head, h, j):
+        rows = pl.ds(h * 128, 128)
+        own = pl.ds(pl.multiple_of((x % 2) * HD, 128), HD)
+        if step == 0:
+            ref = abuf.at[head, y, x // 2, rows, own]
+        elif h == 0:
+            ref = abuf.at[head, y, :, rows]
+        else:
+            ref = abuf.at[head, :, x // 2, rows, own]
+        device = in_plane(0, j) if (step == h) else in_plane(j, 0)
+        send, recv = (b5s, b5r) if step else (a5s, a5r)
+        return copy(ref, ref, send.at[head, h, j - 1], recv.at[head, h, j - 1], device)
+
     allowed = mask[...] > 0.5
     for head in range(HEADS):
         base = head * 3 * HD
@@ -348,77 +451,31 @@
         scores = jnp.where(allowed, scores * (1.0 / math.sqrt(HD)), -1e30)
         weights = jnp.exp(scores - jnp.max(scores, axis=1, keepdims=True))
         soft = (weights / jnp.sum(weights, axis=1, keepdims=True)).astype(BF16)
-        att[:, head * HD : (head + 1) * HD] = jnp.dot(soft, values, preferred_element_type=F32).astype(BF16)
-
-    spread(att, abuf, s4s, s4r)
-    load_o.wait()
-
-    def sum_copy(k, part_of=0):
-        if k == 0:
-            rows = pl.ds(part_of * 128, 128)
-            return copy(send6.at[0, rows], recv6.at[0, rows], s6s.at[0, part_of], s6r.at[0, part_of], along_z(-2 if part_of else 2))
-        by = {1: 1, 2: -1, 3: 2, 4: -2, 5: 1, 6: -1}[k]
-        return copy(send6.at[k], recv6.at[k], s6s.at[k, 0], s6r.at[k, 0], along_z(by))
-
-    for grp in range(5):
-        gather_first(abuf, sems5, s4r, grp)
-    gather_second(abuf, sems5, 0)
-    gather_second(abuf, sems5, 1)
-    gather_last(abuf, sems5, 0)
-    product(abuf, 0, wo, part6, 1)
-    send6[0] = part6[0].astype(BF16)
-    sum_copy(0, 0).start()
-    sum_copy(0, 1).start()
-    gather_second(abuf, sems5, 2)
-    gather_last(abuf, sems5, 1)
-    for k in (1, 2):
-        product(abuf, k, wo, part6, 1)
-        send6[k] = part6[k].astype(BF16)
-        sum_copy(k).start()
-    gather_second(abuf, sems5, 3)
-    gather_last(abuf, sems5, 2)
-    for k in (3, 4):
-        product(abuf, k, wo, part6, 1)
-    gather_second(abuf, sems5, 4)
-    gather_last(abuf, sems5, 3)
-    for k in (5, 6):
-        product(abuf, k, wo, part6, 1)
-        send6[k] = part6[k].astype(BF16)
-        sum_copy(k).start()
-    for k in (3, 4):
-        sum_copy(0, k - 3).wait_recv()
-        sum_copy(k - 2).wait_recv()
-        total = part6[k] + recv6[k - 2].astype(F32)
-        send6[k] = total.astype(BF16)
-        rows = pl.ds((k - 3) * 128, 128)
-        both = part6[k, rows, :] + recv6[k - 2, rows, :].astype(F32) + recv6[0, rows, :].astype(F32)
-        send6[k, rows, :] = both.astype(BF16)
-        sum_copy(k).start()
-    gather_last(abuf, sems5, 4)
-    product(abuf, 7, wo, part6, 1)
-    total = part6[7] + xin[...].astype(F32)
-    for k in (5, 6, 3, 4):
-        sum_copy(k).wait_recv()
-        total = total + recv6[k].astype(F32)
-    result = total.astype(BF16)
-    res[...] = result
-
-    @pl.when(s == 0)
-    def _():
-        hand.start()
-
-    out_ref[0, 0] = result
-
-    spread_drain(xc, xbuf, s1s, s1r)
-    spread_drain(att, abuf, s4s, s4r)
+        ahead = jnp.dot(soft, values, preferred_element_type=F32).astype(BF16)
+        abuf[head, y, x // 2, :, pl.ds(pl.multiple_of((x % 2) * HD, 128), HD)] = ahead
+        for h in range(2):
+            for j in (2, 1, 3):
+                head_copy(0, head, h, j).start()
+
+    @pl.when(first)
+    def _():
+        spread_drain(xc, xbuf, s1s, s1r, 0)
+
+        def stat_drain(i, c):
+            stat_copy(i).wait_send()
+            return c
+
+        lax.fori_loop(1, 16, stat_drain, 0)
+
+    weight_step(3)
+    for head in range(HEADS):
+        for h in range(2):
+            for j in (1, 2, 3):
+                head_copy(0, head, h, j).wait_recv()
+            for j in (2, 1, 3):
+                head_copy(1, head, h, j).start()
+
     gather_drain(xbuf, sems2)
-    gather_drain(abuf, sems5)
-
-    def stat_drain(i, c):
-        stat_copy(i).wait_send()
-        return c
-
-    lax.fori_loop(1, 16, stat_drain, 0)
 
     def csum_drain(i, c):
         csum_copy(i).wait_send()
@@ -428,14 +485,63 @@
     for k in range(7):
         for q in range(4):
             ring_copy(k, q).wait_send()
-    sum_copy(0, 0).wait_send()
-    sum_copy(0, 1).wait_send()
-    for k in range(1, 7):
-        sum_copy(k).wait_send()
-
-    @pl.when(s == 0)
-    def _():
-        hand.wait_send()
+    weight_step(4)
+    for step in range(4):
+        for way in range(2):
+            weight_copy(step, way).wait_send()
+    for head in range(HEADS):
+        for h in range(2):
+            for j in (1, 2, 3):
+                head_copy(0, head, h, j).wait_send()
+
+    @pl.when(s == 1)
+    def _():
+        hand().wait_recv()
+
+    total = xin[...].astype(F32)
+    for head in range(HEADS):
+        for h in range(2):
+            for j in (1, 2, 3):
+                head_copy(1, head, h, j).wait_recv()
+        for d in range(NZ):
+            rows = jnp.concatenate([wo[d, head * HD : head * HD + HD], wo[d, FEAT + head * HD : FEAT + head * HD + HD]], axis=0)
+            total = total + jnp.dot(abuf[head, d // 2, d % 2], rows, preferred_element_type=F32)
+    result = total.astype(BF16)
+    res[...] = result
+
+    @pl.when(first)
+    def _():
+        low, rows = centre(res[...].astype(F32))
+        xc2[...] = low
+        stat2[...] = rows
+
+        @pl.when(far)
+        def _():
+            spread(xc2, xbuf, t1s, s1r, 1, True)
+
+        lax.fori_loop(0, 16, stat_on_send, 0)
+        hand().start()
+
+        @pl.when(jnp.logical_not(far))
+        def _():
+            spread(xc2, xbuf, t1s, s1r, 1, True)
+
+    out_ref[0, 0] = res[...]
+    for head in range(HEADS):
+        for h in range(2):
+            for j in (1, 2, 3):
+                head_copy(1, head, h, j).wait_send()
+
+    @pl.when(first)
+    def _():
+        spread_drain(xc2, xbuf, t1s, s1r, 1, True)
+
+        def stat_on_drain(i, c):
+            stat_on_copy(i).wait_send()
+            return c
+
+        lax.fori_loop(0, 16, stat_on_drain, 0)
+        hand().wait_send()
 
 
 def local(hidden_in, doc_lengths, w_qkv, w_out):
@@ -453,29 +559,27 @@
         scratch_shapes=[
             vmem((LEN, FEAT), BF16),
             vmem((LEN, FEAT), BF16),
+            vmem((LEN, FEAT), BF16),
             vmem((ROWS, COLS), BF16),
-            vmem((ROWS, FEAT), BF16),
+            vmem((NZ, ROWS, FEAT), BF16),
             vmem((16, 8, LEN), F32),
+            vmem((8, LEN), F32),
             vmem((16, 8, COLS), F32),
             vmem((128, LEN), F32),
             vmem((LEN, LEN), F32),
             vmem((LEN, COLS), BF16),
             vmem((LEN, FEAT), BF16),
-            vmem((LEN, FEAT), BF16),
             vmem((8, 4, 64, ROWS), BF16),
-            vmem((8, 4, 64, ROWS), BF16),
+            vmem((HEADS, 4, 2, LEN, 2 * HD), BF16),
             vmem((8, LEN, COLS), F32),
             vmem((7, LEN, COLS), BF16),
             vmem((7, LEN, COLS), BF16),
-            vmem((8, LEN, FEAT), F32),
-            vmem((7, LEN, FEAT), BF16),
-            vmem((7, LEN, FEAT), BF16),
-            dma((3,)), dma((2,)),
-            dma((16,)), dma((8, 2)), dma((16,)), dma((8, 2)),
-            dma((5, 2, 3)), dma((5, 2, 3)), dma((5, 2, 3)), dma((5, 2, 3)),
-            dma((5, 2, 3)), dma((5, 2, 3)), dma((5, 2, 3)), dma((5, 2, 3)),
-            dma((15,)), dma((15,)), dma((7,)), dma((7,)),
-            dma((7, 4)), dma((7, 4)), dma((7, 2)), dma((7, 2)),
+            dma((3,)), dma((2,)), pltpu.SemaphoreType.REGULAR,
+            dma((16,)), dma((8, 2)),
+            dma((5, 2, 3)), dma((5, 2, 3)), dma((5, 2, 3)), dma((5, 2, 3)), dma((15,)), dma((15,)),
+            dma((3, 2, 3)), dma((3, 2, 3)), dma((3, 2, 3)), dma((3, 2, 3)),
+            dma((16,)), dma((15,)), dma((16,)), dma((16,)), dma((7,)), dma((7,)),
+            dma((7, 4)), dma((7, 4)), dma((2, 4)), dma((2, 4)),
         ],
         compiler_params=pltpu.CompilerParams(
             collective_id=0, has_side_effects=True, vmem_limit_bytes=56 * 1024 * 1024

time: 183 us -> 163 us (0.89)
  Pallas kernels: 181 us -> 161 us
    pallas_call x1, Pallas kernels: 181 us -> 161 us  [local(): pl.pallas_call(kernel, out_shape=jax.ShapeDtypeStruct((1, 1, LEN, FEAT),...]
where the time goes in v2:
time: 163 us
  Pallas kernels  161 us (99%)
    pallas_call x1, Pallas kernels, local(): pl.pallas_call(kernel, out_shape=jax.ShapeDtypeStruct((1, 1, LEN, FEAT),...  161 us

profile of v2, /device:TPU:1, one launch (start us, length us, event | category | flops | bytes accessed | tf_op | source)
XLA Modules:
  0.0 162.5 jit_solution(18325577894653791915)
XLA Ops:
  0.0 160.9 %shard_map.46 = bf16[1,1,256,384]{3,2,1,0:T(8,128)(2,1)} custom-call(s32[1,4]{1,0:T(1,128)} %doc_ref.1, bf16[1,256,384]{2,1,0:T(8,128)(2,1)} %hid_ref.1, bf16[1,768,1152]{2,1,0:T(8,128)(2,1)} %wq_hbm.1, bf16[1,768,384]{2,1,0:T(8,128)(2,1)} %wo_hbm.1), custom_call_target="tpu_custom_call" | custom-call | flops 4831838208 | bytes 3145728 | tf_op jit(solution)/shard_map/pallas_call | solution.py:549
  160.9 1.6 copy.6

commit v3 on v2

v3 whole, which is shorter than its diff:
```python
import functools
import math

import jax
import jax.numpy as jnp
from jax import lax
from jax.experimental import pallas as pl
from jax.experimental.pallas import tpu as pltpu
from jax.sharding import PartitionSpec as P

MESH = pl.DeviceIdType.MESH
HD = 128
HEADS = 3
LEN = 256
FEAT = 384
ROWS = 768
COLS = 1152
WIDTH = 6144
NZ = 8
GROUPS = ((0, 1), (1, 2), (3, 2), (5, 2), (7, 1))
F32 = jnp.float32
BF16 = jnp.bfloat16


def kernel(
    doc_ref, hid_ref, wq_hbm, wo_hbm, out_ref,
    xin, wq, wo, turn, norm, mask, proj, res,
    xbuf, abuf, part, send3, recv3,
    load_sem, hand_sem, go_sem,
    t1s, t1r, t2s, s1s, s1r, a2s, a2r, b2s, b2r, a5s, a5r, b5s, b5r,
    s3s, s3r, wos, wor,
):
    s = lax.axis_index("section")
    t = lax.axis_index("tensor")
    z = lax.axis_index("dp")
    y, x = t // 4, t % 4
    first = s == 0

    def along_z(by):
        return (s, t, (z + by + NZ) % NZ)

    def in_plane(dy, dx):
        return (s, ((y + dy) % 4) * 4 + (x + dx) % 4, z)

    def copy(src, dst, send_sem, recv_sem, device):
        return pltpu.make_async_remote_copy(
            src_ref=src, dst_ref=dst, send_sem=send_sem, recv_sem=recv_sem,
            device_id=device, device_id_type=MESH,
        )

    load_q = pltpu.make_async_copy(wq_hbm.at[0], wq, load_sem.at[0])
    load_o = pltpu.make_async_copy(wo_hbm.at[0], wo.at[z], load_sem.at[1])
    load_x = pltpu.make_async_copy(hid_ref.at[0], xin, load_sem.at[2])

    @pl.when(s == 0)
    def _():
        load_x.start()

    load_q.start()
    load_o.start()

    barrier = pltpu.get_barrier_semaphore()

    def greet(device):
        pl.semaphore_signal(barrier, inc=1, device_id=device, device_id_type=MESH)

    def greet_plane(i, c):
        greet(in_plane(i // 4, i % 4))
        return c

    lax.fori_loop(1, 16, greet_plane, 0)

    def greet_line(i, c):
        greet(along_z(i))
        return c

    lax.fori_loop(1, NZ, greet_line, 0)

    @pl.when(s == 1)
    def _():
        def greet_before(i, c):
            greet((0, i, z))
            return c

        lax.fori_loop(0, 16, greet_before, 0)

    def hand():
        return copy(res, xin, hand_sem.at[0], hand_sem.at[1], (1, t, z))

    @pl.when(first)
    def _():
        load_x.wait()

    pl.semaphore_wait(barrier, jnp.where(first, 16, 0) + 15 + 7)

    def turn_copy(src, i, to):
        _, g, _ = in_plane(i // 4, i % 4)
        rows = pl.ds(pl.multiple_of(g * 16, 16), 16)
        cols = pl.ds(pl.multiple_of((t % 2) * FEAT, 128), FEAT)
        sems = t1s if to == 0 else t2s
        return copy(src.at[rows, :], turn.at[t // 2, :, cols], sems.at[i], t1r.at[i], (to, g, z))

    def turn_send(src, to):
        def body(i, c):
            turn_copy(src, i, to).start()
            return c

        lax.fori_loop(1 - to, 16, body, 0)

    def turn_drain(src, to):
        def body(i, c):
            turn_copy(src, i, to).wait_send()
            return c

        lax.fori_loop(1 - to, 16, body, 0)

    own_rows = pl.ds(pl.multiple_of(x * 16, 16), 16)

    def line_copy(k):
        by = (4, -3, 3, -2, 2, -1, 1)[k]
        device = along_z(by)
        return copy(norm.at[device[2]], xbuf.at[k, y, own_rows, :], s1s.at[k], s1r.at[k], device)

    def line_wait(k):
        there = xbuf.at[k, y, own_rows, :]
        pltpu.make_async_copy(there, there, s1r.at[k]).wait()

    def gather_copy(buf, sems, step, grp, h, j):
        k0, n = GROUPS[grp]
        own = pl.ds(pl.multiple_of(x * 16, 16), 16)
        cols = pl.ds(h * FEAT, FEAT)
        if step == 0:
            ref = buf.at[pl.ds(k0, n), y, own, cols]
        elif h == 0:
            ref = buf.at[pl.ds(k0, n), y, :, cols]
        else:
            ref = buf.at[pl.ds(k0, n), :, own, cols]
        device = in_plane(0, j) if (step == h) else in_plane(j, 0)
        return copy(ref, ref, sems[2 * step].at[grp, h, j - 1], sems[2 * step + 1].at[grp, h, j - 1], device)

    def gather_first(buf, sems, grp):
        k0, n = GROUPS[grp]
        for k in range(k0, min(k0 + n, 7)):
            line_wait(k)
        for h in range(2):
            for j in (2, 1, 3):
                gather_copy(buf, sems, 0, grp, h, j).start()

    def gather_second(buf, sems, grp):
        for h in range(2):
            for j in (1, 2, 3):
                gather_copy(buf, sems, 0, grp, h, j).wait_recv()
            for j in (2, 1, 3):
                gather_copy(buf, sems, 1, grp, h, j).start()

    def gather_last(buf, sems, grp):
        for h in range(2):
            for j in (1, 2, 3):
                gather_copy(buf, sems, 1, grp, h, j).wait_recv()

    def gather_drain(buf, sems):
        for grp in range(len(GROUPS)):
            for step in range(2):
                for h in range(2):
                    for j in (1, 2, 3):
                        gather_copy(buf, sems, step, grp, h, j).wait_send()

    @pl.when(first)
    def _():
        rows = pl.ds(pl.multiple_of(t * 16, 16), 16)
        turn[t // 2, :, pl.ds(pl.multiple_of((t % 2) * FEAT, 128), FEAT)] = xin[rows, :]
        turn_send(xin, 0)

    sems2 = (a2s, a2r, b2s, b2r)

    def weight_copy(step, way, part_of):
        chunk = (z + (step if way else -step) + NZ) % NZ
        near = way if part_of == 0 else 1 - way
        ref = wo.at[chunk, pl.ds(near * FEAT, FEAT)]
        return copy(ref, ref, wos.at[way, step, part_of], wor.at[way, step, part_of], along_z(-1 if way else 1))

    def weight_step(step):
        for part_of in range(2):
            for way in range(2):
                if step and (step, part_of) != (3, 1):
                    before = 2 if (step, part_of) == (4, 1) else step - 1
                    weight_copy(before, way, part_of).wait_recv()
                if step < 3 or (step == 3 and part_of == 0):
                    weight_copy(step, way, part_of).start()

    def weight_drain():
        for step in range(4):
            for way in range(2):
                weight_copy(step, way, 0).wait_send()
                if step < 3:
                    weight_copy(step, way, 1).wait_send()

    def product(buf, k, w, into, tiles):
        rows = buf[k].reshape(LEN, ROWS)

        def body(n, c):
            cols = pl.ds(pl.multiple_of(n * FEAT, 128), FEAT)
            into[k, :, cols] = jnp.dot(rows, w[:, cols], preferred_element_type=F32)
            return c

        lax.fori_loop(0, tiles, body, 0)

    def ring_copy(k, q):
        rows = pl.ds(q * 64, 64)
        up = q < 2 if k == 0 else k % 2 == 1
        return copy(send3.at[k, rows], recv3.at[k, rows], s3s.at[k, q], s3r.at[k, q], along_z(1 if up else -1))

    def ring_step(k, q, before):
        rows = pl.ds(q * 64, 64)
        value = part[k, rows, :]
        if before is not None:
            ring_copy(before, q).wait_recv()
            value = value + recv3[before, rows, :].astype(F32)
        send3[k, rows, :] = value.astype(BF16)
        ring_copy(k, q).start()

    @pl.when(s == 1)
    def _():
        pl.semaphore_wait(go_sem, 1)

    load_o.wait()
    weight_step(0)

    for i in range(1, 16):
        turn_copy(xin, i, 0).wait_recv()

    @pl.when(s == 1)
    def _():
        turn_copy(xin, 0, 0).wait_recv()

    whole = turn[...].astype(F32)
    mean = jnp.sum(jnp.sum(whole, axis=0), axis=1, keepdims=True) * (1.0 / WIDTH)
    off = whole - mean[None]
    spread = jnp.sum(jnp.sum(off * off, axis=0), axis=1, keepdims=True) * (1.0 / WIDTH)
    norm[...] = (off * lax.rsqrt(spread + 1e-05)[None]).astype(BF16)
    for k in range(7):
        line_copy(k).start()
    xbuf[7, y, own_rows, :] = norm[z]

    for grp in range(0, 5):
        gather_first(xbuf, sems2, grp)

    weight_step(1)

    row_pos = lax.broadcasted_iota(jnp.int32, (LEN, LEN), 0)
    col_pos = lax.broadcasted_iota(jnp.int32, (LEN, LEN), 1)
    row_doc = jnp.zeros((LEN, LEN), jnp.int32)
    col_doc = jnp.zeros((LEN, LEN), jnp.int32)
    end = jnp.int32(0)
    for i in range(4):
        end = end + doc_ref[0, i]
        row_doc = row_doc + (row_pos >= end).astype(jnp.int32)
        col_doc = col_doc + (col_pos >= end).astype(jnp.int32)
    mask[...] = jnp.where((col_pos <= row_pos) & (row_doc == col_doc), 1.0, 0.0)

    gather_second(xbuf, sems2, 0)
    gather_second(xbuf, sems2, 1)
    load_q.wait()
    gather_last(xbuf, sems2, 0)
    product(xbuf, 0, wq, part, 3)
    for q in (0, 2, 1, 3):
        ring_step(0, q, None)
    gather_second(xbuf, sems2, 2)
    gather_last(xbuf, sems2, 1)
    product(xbuf, 1, wq, part, 3)
    ring_step(1, 2, None)
    ring_step(1, 3, None)
    product(xbuf, 2, wq, part, 3)
    ring_step(2, 0, None)
    ring_step(2, 1, None)
    gather_second(xbuf, sems2, 3)
    gather_last(xbuf, sems2, 2)
    product(xbuf, 3, wq, part, 3)
    product(xbuf, 4, wq, part, 3)
    ring_step(1, 0, 0)
    ring_step(2, 2, 0)
    ring_step(1, 1, 0)
    ring_step(2, 3, 0)
    gather_second(xbuf, sems2, 4)
    gather_last(xbuf, sems2, 3)
    product(xbuf, 5, wq, part, 3)
    product(xbuf, 6, wq, part, 3)
    up_order, down_order = (2, 3, 0, 1), (0, 1, 2, 3)
    for i in range(4):
        ring_step(3, up_order[i], 1)
        ring_step(4, down_order[i], 2)
    gather_last(xbuf, sems2, 4)
    product(xbuf, 7, wq, part, 3)
    for i in range(4):
        ring_step(5, up_order[i], 3)
        ring_step(6, down_order[i], 4)

    weight_step(2)
    for q in range(4):
        rows = pl.ds(q * 64, 64)
        ring_copy(5, q).wait_recv()
        ring_copy(6, q).wait_recv()
        total = part[7, rows, :] + recv3[5, rows, :].astype(F32) + recv3[6, rows, :].astype(F32)
        proj[rows, :] = total.astype(BF16)

    def head_copy(step, head, h, j):
        rows = pl.ds(h * 128, 128)
        own = pl.ds(pl.multiple_of((x % 2) * HD, 128), HD)
        if step == 0:
            ref = abuf.at[head, y, x // 2, rows, own]
        elif h == 0:
            ref = abuf.at[head, y, :, rows]
        else:
            ref = abuf.at[head, :, x // 2, rows, own]
        device = in_plane(0, j) if (step == h) else in_plane(j, 0)
        send, recv = (b5s, b5r) if step else (a5s, a5r)
        return copy(ref, ref, send.at[head, h, j - 1], recv.at[head, h, j - 1], device)

    allowed = mask[...] > 0.5
    for head in range(HEADS):
        base = head * 3 * HD
        query = proj[:, base : base + HD]
        keys = proj[:, base + HD : base + 2 * HD]
        values = proj[:, base + 2 * HD : base + 3 * HD]
        scores = lax.dot_general(query, keys, (((1,), (1,)), ((), ())), preferred_element_type=F32)
        scores = jnp.where(allowed, scores * (1.0 / math.sqrt(HD)), -1e30)
        weights = jnp.exp(scores - jnp.max(scores, axis=1, keepdims=True))
        soft = (weights / jnp.sum(weights, axis=1, keepdims=True)).astype(BF16)
        ahead = jnp.dot(soft, values, preferred_element_type=F32).astype(BF16)
        abuf[head, y, x // 2, :, pl.ds(pl.multiple_of((x % 2) * HD, 128), HD)] = ahead
        for h in range(2):
            for j in (2, 1, 3):
                head_copy(0, head, h, j).start()

    @pl.when(first)
    def _():
        turn_drain(xin, 0)

    for k in range(7):
        line_copy(k).wait_send()
    weight_step(3)
    for head in range(HEADS):
        for h in range(2):
            for j in (1, 2, 3):
                head_copy(0, head, h, j).wait_recv()
            for j in (2, 1, 3):
                head_copy(1, head, h, j).start()

    gather_drain(xbuf, sems2)

    for k in range(7):
        for q in range(4):
            ring_copy(k, q).wait_send()
    weight_step(4)

    @pl.when(first)
    def _():
        pl.semaphore_signal(go_sem, inc=1, device_id=(1, t, z), device_id_type=MESH)

    weight_drain()
    for head in range(HEADS):
        for h in range(2):
            for j in (1, 2, 3):
                head_copy(0, head, h, j).wait_send()

    @pl.when(s == 1)
    def _():
        hand().wait_recv()

    total = xin[...].astype(F32)
    for head in range(HEADS):
        for h in range(2):
            for j in (1, 2, 3):
                head_copy(1, head, h, j).wait_recv()
        for d in range(NZ):
            rows = jnp.concatenate([wo[d, head * HD : head * HD + HD], wo[d, FEAT + head * HD : FEAT + head * HD + HD]], axis=0)
            total = total + jnp.dot(abuf[head, d // 2, d % 2], rows, preferred_element_type=F32)
    result = total.astype(BF16)
    res[...] = result

    @pl.when(first)
    def _():
        turn_send(res, 1)
        hand().start()

    out_ref[0, 0] = res[...]
    for head in range(HEADS):
        for h in range(2):
            for j in (1, 2, 3):
                head_copy(1, head, h, j).wait_send()

    @pl.when(first)
    def _():
        turn_drain(res, 1)
        hand().wait_send()


def local(hidden_in, doc_lengths, w_qkv, w_out):
    vmem, dma = pltpu.VMEM, pltpu.SemaphoreType.DMA
    return pl.pallas_call(
        kernel,
        out_shape=jax.ShapeDtypeStruct((1, 1, LEN, FEAT), BF16),
        in_specs=[
            pl.BlockSpec(memory_space=pltpu.SMEM),
            pl.BlockSpec(memory_space=pl.ANY),
            pl.BlockSpec(memory_space=pl.ANY),
            pl.BlockSpec(memory_space=pl.ANY),
        ],
        out_specs=pl.BlockSpec(memory_space=pltpu.VMEM),
        scratch_shapes=[
            vmem((LEN, FEAT), BF16),
            vmem((ROWS, COLS), BF16),
            vmem((NZ, ROWS, FEAT), BF16),
            vmem((NZ, 16, ROWS), BF16),
            vmem((NZ, 16, ROWS), BF16),
            vmem((LEN, LEN), F32),
            vmem((LEN, COLS), BF16),
            vmem((LEN, FEAT), BF16),
            vmem((8, 4, 64, ROWS), BF16),
            vmem((HEADS, 4, 2, LEN, 2 * HD), BF16),
            vmem((8, LEN, COLS), F32),
            vmem((7, LEN, COLS), BF16),
            vmem((7, LEN, COLS), BF16),
            dma((3,)), dma((2,)), pltpu.SemaphoreType.REGULAR,
            dma((16,)), dma((16,)), dma((16,)), dma((7,)), dma((7,)),
            dma((5, 2, 3)), dma((5, 2, 3)), dma((5, 2, 3)), dma((5, 2, 3)),
            dma((3, 2, 3)), dma((3, 2, 3)), dma((3, 2, 3)), dma((3, 2, 3)),
            dma((7, 4)), dma((7, 4)), dma((2, 4, 2)), dma((2, 4, 2)),
        ],
        compiler_params=pltpu.CompilerParams(
            collective_id=0, has_side_effects=True, vmem_limit_bytes=56 * 1024 * 1024
        ),
        cost_estimate=pl.CostEstimate(
            flops=2 * 2048 * ROWS * (COLS + FEAT), bytes_accessed=3 * 1024 * 1024, transcendentals=3 * LEN * LEN
        ),
    )(doc_lengths, hidden_in, w_qkv, w_out)


def solution(mesh):
    return jax.shard_map(
        local,
        mesh=mesh,
        in_specs=(
            P("dp", None, "tensor"),
            P("dp", None),
            P("section", "dp", "tensor"),
            P("section", "dp", "tensor"),
        ),
        out_specs=P("section", "dp", None, "tensor"),
        check_vma=False,
    )
```

time: 163 us -> 139 us (0.85)
  Pallas kernels: 161 us -> 137 us
    pallas_call x1, Pallas kernels: 161 us -> 137 us  [local(): pl.pallas_call(kernel, out_shape=jax.ShapeDtypeStruct((1, 1, LEN, FEAT),...]
where the time goes in v3:
time: 139 us
  Pallas kernels  137 us (99%)
  local copies, waits for them, and re-layouts  1.62 us (1%)
    pallas_call x1, Pallas kernels, local(): pl.pallas_call(kernel, out_shape=jax.ShapeDtypeStruct((1, 1, LEN, FEAT),...  137 us

profile of v3, /device:TPU:1, one launch (start us, length us, event | category | flops | bytes accessed | tf_op | source)
XLA Modules:
  0.0 138.6 jit_solution(8557359739815055955)
XLA Ops:
  0.0 137.0 %shard_map.46 = bf16[1,1,256,384]{3,2,1,0:T(8,128)(2,1)} custom-call(s32[1,4]{1,0:T(1,128)} %doc_ref.1, bf16[1,256,384]{2,1,0:T(8,128)(2,1)} %hid_ref.1, bf16[1,768,1152]{2,1,0:T(8,128)(2,1)} %wq_hbm.1, bf16[1,768,384]{2,1,0:T(8,128)(2,1)} %wo_hbm.1), custom_call_target="tpu_custom_call" | custom-call | flops 4831838208 | bytes 3145728 | tf_op jit(solution)/shard_map/pallas_call | solution.py:400
  137.0 1.6 %copy.6 = bf16[1,1,256,384]{3,2,1,0:T(8,128)(2,1)} copy(bf16[1,1,256,384]{3,2,1,0:T(8,128)(2,1)} %shard_map.46) | data formatting | bytes 393216

commit v4 on v3

--- a/solution.py
+++ b/solution.py
@@ -205,19 +205,22 @@
 
         lax.fori_loop(0, tiles, body, 0)
 
-    def ring_copy(k, q):
-        rows = pl.ds(q * 64, 64)
-        up = q < 2 if k == 0 else k % 2 == 1
-        return copy(send3.at[k, rows], recv3.at[k, rows], s3s.at[k, q], s3r.at[k, q], along_z(1 if up else -1))
-
-    def ring_step(k, q, before):
-        rows = pl.ds(q * 64, 64)
-        value = part[k, rows, :]
+    def piece(c, r):
+        return pl.ds(r * 128, 128), pl.ds(c * FEAT, FEAT)
+
+    def ring_copy(k, c, r):
+        rows, cols = piece(c, r)
+        up = r == 0 if k == 0 else k % 2 == 1
+        return copy(send3.at[k, rows, cols], recv3.at[k, rows, cols], s3s.at[k, c, r], s3r.at[k, c, r], along_z(1 if up else -1))
+
+    def ring_step(k, c, r, before):
+        rows, cols = piece(c, r)
+        value = part[k, rows, cols]
         if before is not None:
-            ring_copy(before, q).wait_recv()
-            value = value + recv3[before, rows, :].astype(F32)
-        send3[k, rows, :] = value.astype(BF16)
-        ring_copy(k, q).start()
+            ring_copy(before, c, r).wait_recv()
+            value = value + recv3[before, rows, cols].astype(F32)
+        send3[k, rows, cols] = value.astype(BF16)
+        ring_copy(k, c, r).start()
 
     @pl.when(s == 1)
     def _():
@@ -263,46 +266,38 @@
     load_q.wait()
     gather_last(xbuf, sems2, 0)
     product(xbuf, 0, wq, part, 3)
-    for q in (0, 2, 1, 3):
-        ring_step(0, q, None)
+    for c in range(3):
+        ring_step(0, c, 0, None)
+        ring_step(0, c, 1, None)
     gather_second(xbuf, sems2, 2)
     gather_last(xbuf, sems2, 1)
     product(xbuf, 1, wq, part, 3)
-    ring_step(1, 2, None)
-    ring_step(1, 3, None)
+    for c in range(3):
+        ring_step(1, c, 1, None)
     product(xbuf, 2, wq, part, 3)
-    ring_step(2, 0, None)
-    ring_step(2, 1, None)
+    for c in range(3):
+        ring_step(2, c, 0, None)
     gather_second(xbuf, sems2, 3)
     gather_last(xbuf, sems2, 2)
     product(xbuf, 3, wq, part, 3)
     product(xbuf, 4, wq, part, 3)
-    ring_step(1, 0, 0)
-    ring_step(2, 2, 0)
-    ring_step(1, 1, 0)
-    ring_step(2, 3, 0)
+    for c in range(3):
+        ring_step(1, c, 0, 0)
+        ring_step(2, c, 1, 0)
     gather_second(xbuf, sems2, 4)
     gather_last(xbuf, sems2, 3)
     product(xbuf, 5, wq, part, 3)
     product(xbuf, 6, wq, part, 3)
-    up_order, down_order = (2, 3, 0, 1), (0, 1, 2, 3)
-    for i in range(4):
-        ring_step(3, up_order[i], 1)
-        ring_step(4, down_order[i], 2)
+    for c, r in ((0, 1), (1, 1), (0, 0), (2, 1), (1, 0), (2, 0)):
+        ring_step(3, c, r, 1)
+        ring_step(4, c, 1 - r, 2)
     gather_last(xbuf, sems2, 4)
     product(xbuf, 7, wq, part, 3)
-    for i in range(4):
-        ring_step(5, up_order[i], 3)
-        ring_step(6, down_order[i], 4)
+    for c, r in ((0, 1), (0, 0), (1, 1), (1, 0), (2, 1), (2, 0)):
+        ring_step(5, c, r, 3)
+        ring_step(6, c, 1 - r, 4)
 
     weight_step(2)
-    for q in range(4):
-        rows = pl.ds(q * 64, 64)
-        ring_copy(5, q).wait_recv()
-        ring_copy(6, q).wait_recv()
-        total = part[7, rows, :] + recv3[5, rows, :].astype(F32) + recv3[6, rows, :].astype(F32)
-        proj[rows, :] = total.astype(BF16)
-
     def head_copy(step, head, h, j):
         rows = pl.ds(h * 128, 128)
         own = pl.ds(pl.multiple_of((x % 2) * HD, 128), HD)
@@ -319,6 +314,11 @@
     allowed = mask[...] > 0.5
     for head in range(HEADS):
         base = head * 3 * HD
+        for r in (1, 0):
+            ring_copy(5, head, r).wait_recv()
+            ring_copy(6, head, 1 - r).wait_recv()
+        cols = pl.ds(base, FEAT)
+        proj[:, cols] = (part[7, :, cols] + recv3[5, :, cols].astype(F32) + recv3[6, :, cols].astype(F32)).astype(BF16)
         query = proj[:, base : base + HD]
         keys = proj[:, base + HD : base + 2 * HD]
         values = proj[:, base + 2 * HD : base + 3 * HD]
@@ -338,8 +338,9 @@
 
     for k in range(7):
         line_copy(k).wait_send()
-    weight_step(3)
     for head in range(HEADS):
+        if head == HEADS - 1:
+            weight_step(3)
         for h in range(2):
             for j in (1, 2, 3):
                 head_copy(0, head, h, j).wait_recv()
@@ -349,8 +350,9 @@
     gather_drain(xbuf, sems2)
 
     for k in range(7):
-        for q in range(4):
-            ring_copy(k, q).wait_send()
+        for c in range(3):
+            ring_copy(k, c, 0).wait_send()
+            ring_copy(k, c, 1).wait_send()
     weight_step(4)
 
     @pl.when(first)
@@ -425,7 +427,7 @@
             dma((16,)), dma((16,)), dma((16,)), dma((7,)), dma((7,)),
             dma((5, 2, 3)), dma((5, 2, 3)), dma((5, 2, 3)), dma((5, 2, 3)),
             dma((3, 2, 3)), dma((3, 2, 3)), dma((3, 2, 3)), dma((3, 2, 3)),
-            dma((7, 4)), dma((7, 4)), dma((2, 4, 2)), dma((2, 4, 2)),
+            dma((7, 3, 2)), dma((7, 3, 2)), dma((2, 4, 2)), dma((2, 4, 2)),
         ],
         compiler_params=pltpu.CompilerParams(
             collective_id=0, has_side_effects=True, vmem_limit_bytes=56 * 1024 * 1024

time: 139 us -> 133 us (0.957)
  Pallas kernels: 137 us -> 131 us
    pallas_call x1, Pallas kernels: 137 us -> 131 us  [local(): pl.pallas_call(kernel, out_shape=jax.ShapeDtypeStruct((1, 1, LEN, FEAT),...]
where the time goes in v4:
time: 133 us
  Pallas kernels  131 us (98%)
  local copies, waits for them, and re-layouts  1.62 us (1%)
    pallas_call x1, Pallas kernels, local(): pl.pallas_call(kernel, out_shape=jax.ShapeDtypeStruct((1, 1, LEN, FEAT),...  131 us

profile of v4, /device:TPU:1, one launch (start us, length us, event | category | flops | bytes accessed | tf_op | source)
XLA Modules:
  0.0 132.6 jit_solution(6601904115190636693)
XLA Ops:
  0.0 131.0 %shard_map.46 = bf16[1,1,256,384]{3,2,1,0:T(8,128)(2,1)} custom-call(s32[1,4]{1,0:T(1,128)} %doc_ref.1, bf16[1,256,384]{2,1,0:T(8,128)(2,1)} %hid_ref.1, bf16[1,768,1152]{2,1,0:T(8,128)(2,1)} %wq_hbm.1, bf16[1,768,384]{2,1,0:T(8,128)(2,1)} %wo_hbm.1), custom_call_target="tpu_custom_call" | custom-call | flops 4831838208 | bytes 3145728 | tf_op jit(solution)/shard_map/pallas_call | solution.py:402
  131.0 1.6 %copy.6 = bf16[1,1,256,384]{3,2,1,0:T(8,128)(2,1)} copy(bf16[1,1,256,384]{3,2,1,0:T(8,128)(2,1)} %shard_map.46) | data formatting | bytes 393216

commit v5 on v4

--- a/solution.py
+++ b/solution.py
@@ -285,10 +285,13 @@
         ring_step(1, c, 0, 0)
         ring_step(2, c, 1, 0)
     gather_second(xbuf, sems2, 4)
+    for c, r in ((0, 1), (1, 1), (0, 0)):
+        ring_step(3, c, r, 1)
+        ring_step(4, c, 1 - r, 2)
     gather_last(xbuf, sems2, 3)
     product(xbuf, 5, wq, part, 3)
     product(xbuf, 6, wq, part, 3)
-    for c, r in ((0, 1), (1, 1), (0, 0), (2, 1), (1, 0), (2, 0)):
+    for c, r in ((2, 1), (1, 0), (2, 0)):
         ring_step(3, c, r, 1)
         ring_step(4, c, 1 - r, 2)
     gather_last(xbuf, sems2, 4)

time: 133 us -> 133 us (level)
  no operation moved by 1% of the time
where the time goes in v5:
time: 133 us
  Pallas kernels  131 us (98%)
  local copies, waits for them, and re-layouts  1.62 us (1%)
    pallas_call x1, Pallas kernels, local(): pl.pallas_call(kernel, out_shape=jax.ShapeDtypeStruct((1, 1, LEN, FEAT),...  131 us

profile of v5, /device:TPU:1, one launch (start us, length us, event | category | flops | bytes accessed | tf_op | source)
XLA Modules:
  0.0 132.5 jit_solution(17528071264761277495)
XLA Ops:
  0.0 130.9 %shard_map.46 = bf16[1,1,256,384]{3,2,1,0:T(8,128)(2,1)} custom-call(s32[1,4]{1,0:T(1,128)} %doc_ref.1, bf16[1,256,384]{2,1,0:T(8,128)(2,1)} %hid_ref.1, bf16[1,768,1152]{2,1,0:T(8,128)(2,1)} %wq_hbm.1, bf16[1,768,384]{2,1,0:T(8,128)(2,1)} %wo_hbm.1), custom_call_target="tpu_custom_call" | custom-call | flops 4831838208 | bytes 3145728 | tf_op jit(solution)/shard_map/pallas_call | solution.py:405
  130.9 1.6 %copy.6 = bf16[1,1,256,384]{3,2,1,0:T(8,128)(2,1)} copy(bf16[1,1,256,384]{3,2,1,0:T(8,128)(2,1)} %shard_map.46) | data formatting | bytes 393216
